TPU v7x, 512 devices: a whole 4x8x8 slice. The times are simulated.
512 devices in a mesh: dp: 8 (over y), ctx: 64 (over z, x, core).
Axes of the slice: x: 4, y: 8, z: 8, core: 2. Of those that a mesh axis runs over, the one named last changes fastest.
Arguments:
- query: bfloat16 [8, 16384, 1024], P('dp', 'ctx'), may hold values from -6 to 6
- keys: bfloat16 [8, 16384, 1024], P('dp', 'ctx'), may hold values from -6 to 6
- values: bfloat16 [8, 16384, 1024], P('dp', 'ctx'), may hold values from -6 to 6
- cotangent: bfloat16 [8, 16384, 1024], P('dp', 'ctx'), may hold values from -16 to 16
- out_weight: bfloat16 [1024, 1024], P('dp'), may hold values from -0.1875 to 0.1875
Outputs:
- query_grad: bfloat16 [8, 16384, 1024], P('dp', 'ctx')
- derivative_of_keys: bfloat16 [8, 16384, 1024], P('dp', 'ctx')
- derivative_of_values: bfloat16 [8, 16384, 1024], P('dp', 'ctx')
- weight_grad: float32 [1024, 1024], P(('dp', 'ctx'))
All inputs are finite; a program needn't handle non-finite values.
Results may differ from a plain program's by a relative error of at most 0.015.
Values may be sent and summed in bfloat16 or wider, within the bound.
No kernel may reach another device: no remote copies, remote signals or barrier semaphores. Data moves between devices by JAX's collectives and lax.ppermute only.
A program may use at most 192 MiB of HBM per device.

v0:
```python
import math

import jax
import jax.numpy as jnp
from jax import lax
from jax.sharding import PartitionSpec as P

HEAD = 128


def entering(shard, axis, combine, identity, reverse):
    size, here = (lax.axis_size(axis), lax.axis_index(axis))
    everything = lax.all_gather(shard.astype(jnp.bfloat16), axis)
    start = jnp.broadcast_to(jnp.asarray(identity, shard.dtype), shard.shape)

    def turn(k, before):
        at = size - 1 - k if reverse else k
        reached = at > here if reverse else at < here
        new = combine(before, everything[at].astype(shard.dtype))
        return jnp.where(reached, new, before)

    return lax.fori_loop(0, size, turn, start)


def add_states(earlier, later_part):
    return earlier + later_part


def per_device(query, keys, values, cotangent, out_weight):
    stretch = query.shape[1]
    width = query.shape[2]
    head_count = width // HEAD
    ctx_count = lax.axis_size("ctx")
    dp_count = lax.axis_size("dp")
    seq_len = stretch * ctx_count
    factor = 1.0 / math.sqrt(HEAD * seq_len)
    grad_factor = 1.0 / math.sqrt(dp_count * seq_len)
    tokens_dy = cotangent[0]
    d_out = jnp.dot(
        tokens_dy,
        lax.all_gather(out_weight, "dp", axis=0, tiled=True),
        preferred_element_type=jnp.float32,
    ).astype(jnp.bfloat16)
    shape3 = (stretch, head_count, HEAD)
    local_query_rows = query[0].reshape(shape3)
    device_keys_slice = keys[0].reshape(shape3)
    local_value_rows = values[0].reshape(shape3)
    local_output_rows = d_out.reshape(shape3)
    running_state_list = jnp.einsum(
        "ptq,pto->tqo", device_keys_slice, local_value_rows, preferred_element_type=jnp.float32
    )
    state_gradient_list = jnp.einsum(
        "ptq,pto->tqo", local_query_rows, local_output_rows, preferred_element_type=jnp.float32
    )
    zeros_state = jnp.zeros_like(running_state_list)
    prior = entering(running_state_list, "ctx", add_states, zeros_state, False)
    later = entering(state_gradient_list, "ctx", add_states, zeros_state, True)
    first_half_rows = prior.astype(jnp.bfloat16)
    latter_portion_tokens = later.astype(jnp.bfloat16)
    token_positions = jnp.arange(stretch, dtype=jnp.int32)
    masked_future = token_positions[:, None] >= token_positions[None, :]
    raw_scores = jnp.einsum(
        "thd,shd->hts", local_query_rows, device_keys_slice, preferred_element_type=jnp.float32
    )
    scores = jnp.where(masked_future, factor * raw_scores, 0.0).astype(jnp.bfloat16)
    output = jnp.einsum(
        "hts,shv->thv", scores, local_value_rows, preferred_element_type=jnp.float32
    )
    output = output + factor * jnp.einsum(
        "gqr,qrx->gqx", local_query_rows, first_half_rows, preferred_element_type=jnp.float32
    )
    output = output.reshape(stretch, width).astype(jnp.bfloat16)
    raw_grad = jnp.einsum(
        "thv,shv->hts", local_output_rows, local_value_rows, preferred_element_type=jnp.float32
    )
    score_grad = jnp.where(masked_future, factor * raw_grad, 0.0).astype(jnp.bfloat16)
    q_grad = jnp.einsum(
        "hts,shk->thk", score_grad, device_keys_slice, preferred_element_type=jnp.float32
    )
    q_grad = q_grad + factor * jnp.einsum(
        "mod,oad->moa", local_output_rows, first_half_rows, preferred_element_type=jnp.float32
    )
    k_grad = jnp.einsum(
        "hts,thk->shk", score_grad, local_query_rows, preferred_element_type=jnp.float32
    )
    k_grad = k_grad + factor * jnp.einsum(
        "jqn,qxn->jqx", local_value_rows, latter_portion_tokens, preferred_element_type=jnp.float32
    )
    v_grad = jnp.einsum(
        "hts,thv->shv", scores, local_output_rows, preferred_element_type=jnp.float32
    )
    v_grad = v_grad + factor * jnp.einsum(
        "pld,ldu->plu", device_keys_slice, latter_portion_tokens, preferred_element_type=jnp.float32
    )
    partial_full = lax.dot_general(
        tokens_dy, output, (((0,), (0,)), ((), ())), preferred_element_type=jnp.float32
    )
    weight_grad = (
        lax.psum_scatter(partial_full, ("dp", "ctx"), scatter_dimension=0, tiled=True) * grad_factor
    )
    return (
        q_grad.reshape(1, stretch, width).astype(jnp.bfloat16),
        k_grad.reshape(1, stretch, width).astype(jnp.bfloat16),
        v_grad.reshape(1, stretch, width).astype(jnp.bfloat16),
        weight_grad,
    )


def solution(mesh):
    placed = (
        P("dp", "ctx", None),
        P("dp", "ctx", None),
        P("dp", "ctx", None),
        P("dp", "ctx", None),
        P("dp", None),
    )
    return jax.shard_map(
        per_device,
        mesh=mesh,
        in_specs=placed,
        out_specs=(
            P("dp", "ctx", None),
            P("dp", "ctx", None),
            P("dp", "ctx", None),
            P(("dp", "ctx"), None),
        ),
        check_vma=False,
    )
```

profile of v0, /device:TPU:1, one launch (start us, length us, event | category | flops | bytes accessed | tf_op | source)
XLA Modules:
  0.0 690.3 jit_solution(17402351801938360833)
XLA Ops:
  7.2 1.3 copy.60
  13.2 1.5 convolution_bitcast_fusion.2
  14.7 109.1 %all-gather.8.cloned.1.call-done = bf16[512,128,128]{2,1,0:T(8,128)(2,1)} async-done(((bf16[8,128,128]{2,1,0:T(8,128)(2,1)}), bf16[512,128,128]{2,1,0:T(8,128)(2,1)}) %all-gather.8.cloned.1.call-update) | async-done | bytes 16777232 | tf_op jit(solution)/shard_map/all_gather | solution.py:13
  123.8 80.5 %while.30 = (s32[]{:T(128)}, f32[8,128,128]{2,1,0:T(8,128)S(1)}, s32[]{:T(128)}, bf16[64,8,128,128]{3,2,1,0:T(8,128)(2,1)}, s32[]{:T(128)}, /*index=5*/s32[]{:T(128)}) while((s32[]{:T(128)}, f32[8,128,128]{2,1,0:T(8,128)S(1)}, s32[]{:T(128)}, bf16[64,8,128,128]{3,2,1,0:T(8,128)(2,1)}, s32[]{:T(128)}, /*index=5*/s32[]{:T(128)}) %tuple.89), condition=%wide.region_1.2_spmd.clone, body=%wide.region_0.1_spmd.clone.sunk | while | flops 524292 | bytes 1310821 | solution.py:22
  125.1 1.2 add_select_fusion.4
  126.3 1.2 add_select_fusion.4
  127.6 1.2 add_select_fusion.4
  130.1 1.2 add_select_fusion.4
  131.4 1.2 add_select_fusion.4
  132.6 1.2 add_select_fusion.4
  133.9 1.2 add_select_fusion.4
  136.4 1.2 add_select_fusion.4
  137.7 1.2 add_select_fusion.4
  138.9 1.2 add_select_fusion.4
  140.2 1.2 add_select_fusion.4
  141.4 1.2 add_select_fusion.4
  142.7 1.2 add_select_fusion.4
  144.0 1.2 add_select_fusion.4
  145.2 1.2 add_select_fusion.4
  146.5 1.2 add_select_fusion.4
  147.7 1.2 add_select_fusion.4
  149.0 1.2 add_select_fusion.4
  150.2 1.2 add_select_fusion.4
  151.5 1.2 add_select_fusion.4
  152.8 1.2 add_select_fusion.4
  154.0 1.2 add_select_fusion.4
  155.3 1.2 add_select_fusion.4
  156.6 1.2 add_select_fusion.4
  157.8 1.2 add_select_fusion.4
  159.1 1.2 add_select_fusion.4
  160.3 1.2 add_select_fusion.4
  161.6 1.2 add_select_fusion.4
  162.9 1.2 add_select_fusion.4
  164.1 1.2 add_select_fusion.4
  166.6 1.2 add_select_fusion.4
  167.9 1.2 add_select_fusion.4
  169.1 1.2 add_select_fusion.4
  170.4 1.2 add_select_fusion.4
  171.7 1.2 add_select_fusion.4
  172.9 1.2 add_select_fusion.4
  175.4 1.2 add_select_fusion.4
  176.7 1.2 add_select_fusion.4
  177.9 1.2 add_select_fusion.4
  179.2 1.2 add_select_fusion.4
  181.7 1.2 add_select_fusion.4
  183.0 1.2 add_select_fusion.4
  184.2 1.2 add_select_fusion.4
  185.5 1.2 add_select_fusion.4
  186.7 1.2 add_select_fusion.4
  188.0 1.2 add_select_fusion.4
  190.5 1.2 add_select_fusion.4
  204.3 1.6 fusion.10
  205.9 2.7 convolution_bitcast_fusion
  208.7 3.1 convolution_convert_fusion
  211.8 1.2 copy.59
  214.3 1.5 select_convert_fusion.1
  216.3 1.4 convolution_bitcast_fusion.1
  217.7 1.3 fusion.26
  220.4 270.3 %all-reduce.3.cloned.1.call-done = f32[1024,1024]{0,1:T(8,128)} async-done(((f32[1024,1024]{0,1:T(8,128)}), f32[1024,1024]{0,1:T(8,128)}) %all-reduce.3.cloned.1.call-update) | async-done | bytes 4194320
  490.6 1.2 dynamic-slice_multiply_fusion
  492.7 104.6 %all-gather.10.cloned.1.call-done = bf16[512,128,128]{2,1,0:T(8,128)(2,1)} async-done(((bf16[8,128,128]{2,1,0:T(8,128)(2,1)}), bf16[512,128,128]{2,1,0:T(8,128)(2,1)}) %all-gather.10.cloned.1.call-update) | async-done | bytes 16777232 | tf_op jit(solution)/shard_map/all_gather | solution.py:13
  597.2 80.7 %while.31 = (s32[]{:T(128)}, f32[8,128,128]{2,1,0:T(8,128)S(1)}, s32[]{:T(128)}, bf16[64,8,128,128]{3,2,1,0:T(8,128)(2,1)}, s32[]{:T(128)}, /*index=5*/s32[]{:T(128)}, s32[]{:T(128)}, s32[]{:T(128)}) while((s32[]{:T(128)}, f32[8,128,128]{2,1,0:T(8,128)S(1)}, s32[]{:T(128)}, bf16[64,8,128,128]{3,2,1,0:T(8,128)(2,1)}, s32[]{:T(128)}, ...), condition=%wide.region_3.4_spmd.clone, body=%wide.region_2.3_spmd.clone.sunk | while | flops 524296 | bytes 1310883 | solution.py:22
  678.0 2.4 fusion.8
  680.4 2.0 copy.52
  (119 shorter events, 109.8 us)
Async XLA Ops:
  7.2 198.8 %copy-start = (bf16[1,256,1024]{2,1,0:T(8,128)(2,1)S(1)}, bf16[1,256,1024]{2,1,0:T(8,128)(2,1)}, u32[]{:S(2)}) copy-start(bf16[1,256,1024]{2,1,0:T(8,128)(2,1)} %param.12) | copy-start | bytes 1572868
  7.2 4.5 copy-start.6
  7.2 116.6 %all-gather.8.cloned.1.call-start = ((), (), s32[]{:S(2)}) async-start(), calls=%async_computation.1 | async-start | bytes 17039360 | tf_op jit(solution)/shard_map/all_gather | solution.py:13
  10.8 197.9 %all-gather.6.cloned.1.call-start = ((), (), s32[]{:S(2)}) async-start(), calls=%async_computation | async-start | bytes 2359296 | tf_op jit(solution)/shard_map/all_gather | solution.py:41
  11.5 479.1 %all-reduce.3.cloned.1.call-start = ((), (), s32[]{:S(2)}) async-start(), calls=%async_computation.3 | async-start | bytes 8388608
  12.3 1.0 copy-start.3
  208.6 388.6 %all-gather.10.cloned.1.call-start = ((), (), s32[]{:S(2)}) async-start(), calls=%async_computation.2 | async-start | bytes 17039360 | tf_op jit(solution)/shard_map/all_gather | solution.py:13
  213.1 1.2 copy-start.1
  215.8 1.9 copy-start.2
  215.8 1.9 copy-start.4
  678.0 4.4 copy-start.5
Sparse Core Ops, SparseCore 0:
  11.9 111.8 all-gather.7
  125.9 35.9 all-gather.5
  208.8 281.8 all-reduce.2
  494.4 102.7 all-gather.9
where the time goes:
time: 695 us; the launch traced here: 690 us
  waiting for transfers between devices  485 us (70%)
  other arithmetic  159 us (23%)
  matrix products  18.5 us (3%)
  between operations  14 us (2%)
  local copies, waits for them, and re-layouts  10.5 us (2%)
    unnamed x5, waiting for transfers between devices  271 us
    all_gather x2, waiting for transfers between devices, entering(): everything = lax.all_gather(shard.astype(jnp.bfloat16), axis)  214 us
    select_n x128, other arithmetic, turn(): return jnp.where(reached, new, before)  158 us
  transfers between devices with their start and end apart: 4, of which 3 were waited for; matrix products, arithmetic and copies ran while one was open for 14% of the time, Pallas kernels for 0%

commit v1 on v0

v1 whole, which is shorter than its diff:
```python
import functools
import math

import jax
import jax.numpy as jnp
from jax import lax
from jax.experimental import pallas as pl
from jax.experimental.pallas import tpu as pltpu
from jax.sharding import Mesh, PartitionSpec as P

HEAD = 128
F32 = jnp.float32
BF16 = jnp.bfloat16


def dot(a, b, contract):
    return lax.dot_general(a, b, ((contract[:1], contract[1:]), ((), ())), preferred_element_type=F32)


def head(ref, h):
    return ref[:, h * HEAD : (h + 1) * HEAD]


def call(kernel, core, ins, outs, **cost):
    def spec(operand):
        if isinstance(operand, tuple):
            rows, columns = operand[0].shape
            return pl.BlockSpec((rows, columns // 2), lambda i, c: (0, c[0]))
        return pl.BlockSpec(operand.shape, lambda i, c, n=operand.ndim: (0,) * n)

    arrays = [operand[0] if isinstance(operand, tuple) else operand for operand in ins]
    return pl.pallas_call(
        kernel,
        grid_spec=pltpu.PrefetchScalarGridSpec(
            num_scalar_prefetch=1,
            grid=(1,),
            in_specs=[spec(operand) for operand in ins],
            out_specs=[pl.BlockSpec(o.shape, lambda i, c, n=len(o.shape): (0,) * n) for o in outs],
        ),
        out_shape=outs,
        compiler_params=pltpu.CompilerParams(vmem_limit_bytes=48 * 1024 * 1024),
    )(core, *arrays)


def shape(dims, dtype):
    return jax.ShapeDtypeStruct(dims, dtype)


def states_kernel(core, k, v, kv_far, near, far, both):
    for h in range(near.shape[0]):
        mine = dot(head(k, h), head(v, h), (0, 0))
        other = dot(head(kv_far.at[0], h), head(kv_far.at[1], h), (0, 0))
        near[h] = mine
        far[h] = other
        both[h] = (mine + other).astype(BF16)


def prefix_kernel(reverse, core, terms, sums):
    count = terms.shape[0]
    total = jnp.zeros(terms.shape[1:], F32)
    for k in reversed(range(count)) if reverse else range(count):
        sums[k] = total.astype(BF16)
        total = total + terms[k].astype(F32)


def masked(scores, factor):
    rows = lax.broadcasted_iota(jnp.int32, scores.shape, 0)
    columns = lax.broadcasted_iota(jnp.int32, scores.shape, 1)
    return jnp.where(rows >= columns, factor * scores, 0.0).astype(BF16)


def entering(chunk, inside, here):
    return (chunk.astype(F32) + jnp.where(here, inside, 0.0)).astype(BF16)


def output_kernel(factor, core, q, k, v, q_far, kv_far, dy, dy_far, prior, s_near, s_far, weight, out, out_far):
    for h in range(s_near.shape[0]):
        for qs, ks, vs, inside, here, o in (
            (q, k, v, s_far, core[0] == 1, out),
            (q_far, kv_far.at[0], kv_far.at[1], s_near, core[0] == 0, out_far),
        ):
            qh = head(qs, h)
            before = entering(prior[h], inside[h], here)
            scores = masked(dot(qh, head(ks, h), (1, 1)), factor)
            o[:, h * HEAD : (h + 1) * HEAD] = (
                dot(scores, head(vs, h), (1, 0)) + factor * dot(qh, before, (1, 0))
            ).astype(BF16)
    weight[...] = (dot(dy[...], out[...], (0, 0)) + dot(dy_far[...], out_far[...], (0, 0))).astype(BF16)


def d_out_kernel(core, dy, dy_far, w, q, q_far, d, d_far, near, far, both):
    d[...] = dot(dy[...], w[...], (1, 0)).astype(BF16)
    d_far[...] = dot(dy_far[...], w[...], (1, 0)).astype(BF16)
    for h in range(near.shape[0]):
        mine = dot(head(q, h), head(d, h), (0, 0))
        other = dot(head(q_far, h), head(d_far, h), (0, 0))
        near[h] = mine
        far[h] = other
        both[h] = (mine + other).astype(BF16)


def grads_kernel(
    factor, core, q, k, v, q_far, kv_far, d, d_far, prior, s_near, s_far, later, g_near, g_far, near, far
):
    first = core[0] == 0
    for h in range(s_near.shape[0]):
        at = slice(h * HEAD, (h + 1) * HEAD)
        for qs, ks, vs, ds, s_in, s_here, g_in, g_here, o in (
            (q, k, v, d, s_far, core[0] == 1, g_far, first, near),
            (q_far, kv_far.at[0], kv_far.at[1], d_far, s_near, first, g_near, core[0] == 1, far),
        ):
            qh, kh, vh, dh = head(qs, h), head(ks, h), head(vs, h), head(ds, h)
            before = entering(prior[h], s_in[h], s_here)
            after = entering(later[h], g_in[h], g_here)
            scores = masked(dot(qh, kh, (1, 1)), factor)
            score_grad = masked(dot(dh, vh, (1, 1)), factor)
            o[0, :, at] = (dot(score_grad, kh, (1, 0)) + factor * dot(dh, before, (1, 1))).astype(BF16)
            o[1, :, at] = (dot(score_grad, qh, (0, 0)) + factor * dot(vh, after, (1, 1))).astype(BF16)
            o[2, :, at] = (dot(scores, dh, (0, 0)) + factor * dot(kh, after, (1, 0))).astype(BF16)


def join_kernel(core, near, far, q_grad, k_grad, v_grad):
    width = near.shape[2]
    for i, o in enumerate((q_grad, k_grad, v_grad)):

        @pl.when(core[0] == 0)
        def _():
            o[:, :width] = near[i]
            o[:, width:] = far[i]

        @pl.when(core[0] == 1)
        def _():
            o[:, :width] = far[i]
            o[:, width:] = near[i]


def sum_kernel(scale, core, parts, total):
    count, rows, columns = parts.shape
    halves = [jnp.zeros((rows, columns), F32), jnp.zeros((rows, columns), F32)]
    for k in range(count):
        halves[k % 2] = halves[k % 2] + parts[k].astype(F32)
    total[:, :columns] = halves[0] * scale
    total[:, columns:] = halves[1] * scale


def per_device(query, keys, values, cotangent, out_weight):
    q, k, v, dy = query[0], keys[0], values[0], cotangent[0]
    stretch, width = q.shape
    half = width // 2
    heads = half // HEAD
    sizes = {axis: lax.axis_size(axis) for axis in ("y", "z", "x", "c")}
    chips = sizes["z"] * sizes["x"]
    seq_len = stretch * chips * 2
    factor = 1.0 / math.sqrt(HEAD * seq_len)
    grad_factor = 1.0 / math.sqrt(sizes["y"] * seq_len)
    c = lax.axis_index("c")
    core = c.reshape(1).astype(jnp.int32)

    def halves(a, index):
        return lax.dynamic_slice_in_dim(a, index * half, half, 1)

    def swap(a):
        return lax.ppermute(a, "c", ((0, 1), (1, 0)))

    w = lax.all_gather(halves(out_weight, c), "y", axis=0, tiled=True)
    kv_far = swap(jnp.stack([halves(k, 1 - c), halves(v, 1 - c)]))
    q_dy_far = swap(jnp.concatenate([halves(q, 1 - c), dy], 1))
    q_far, dy_far = q_dy_far[:, :half], q_dy_far[:, half:]

    def scan(both, reverse):
        slices = both.reshape(chips, heads * HEAD // chips, HEAD)
        slices = lax.all_to_all(slices, ("z", "x"), 0, 0)
        (sums,) = call(functools.partial(prefix_kernel, reverse), core, [slices], [shape(slices.shape, BF16)])
        return lax.all_to_all(sums, ("z", "x"), 0, 0).reshape(heads, HEAD, HEAD)

    states = [shape((heads, HEAD, HEAD), t) for t in (F32, F32, BF16)]
    tokens = shape((stretch, half), BF16)

    s_near, s_far, s_both = call(states_kernel, core, [(k, 0), (v, 0), kv_far], states)
    prior = scan(s_both, False)
    partial, _, _ = call(
        functools.partial(output_kernel, factor),
        core,
        [(q, 0), (k, 0), (v, 0), q_far, kv_far, dy, dy_far, prior, s_near, s_far],
        [shape((width, half), BF16), tokens, tokens],
    )
    scattered = lax.psum_scatter(partial, "y", scatter_dimension=0, tiled=True)

    d, d_far, g_near, g_far, g_both = call(
        d_out_kernel, core, [dy, dy_far, w, (q, 0), q_far], [tokens, tokens] + states
    )
    later = scan(g_both, True)
    grads = shape((3, stretch, half), BF16)
    near, far = call(
        functools.partial(grads_kernel, factor),
        core,
        [(q, 0), (k, 0), (v, 0), q_far, kv_far, d, d_far, prior, s_near, s_far, later, g_near, g_far],
        [grads, grads],
    )
    back = swap(far)
    whole = shape((stretch, width), BF16)
    q_grad, k_grad, v_grad = call(join_kernel, core, [near, back], [whole] * 3)

    rows = width // sizes["y"] // (chips * 2)
    parts = lax.all_to_all(scattered.reshape(chips * 2, rows, half), ("z", "x", "c"), 0, 0)
    (weight_grad,) = call(functools.partial(sum_kernel, grad_factor), core, [parts], [shape((rows, width), F32)])
    return q_grad[None], k_grad[None], v_grad[None], weight_grad


def solution(mesh):
    dp, ctx = mesh.devices.shape
    chips = Mesh(mesh.devices.reshape(dp, ctx // 8, 4, 2), ("y", "z", "x", "c"))
    tokens = P("y", ("z", "x", "c"), None)
    return jax.shard_map(
        per_device,
        mesh=chips,
        in_specs=(tokens, tokens, tokens, tokens, P("y", None)),
        out_specs=(tokens, tokens, tokens, P(("y", "z", "x", "c"), None)),
        check_vma=False,
    )
```

time: 695 us -> 132 us (0.19)
  waiting for transfers between devices: 485 us -> 15.4 us
  other arithmetic: 159 us -> 1 us
  blocking collectives: 0 us -> 41.7 us
  starting transfers between devices: 0.16 us -> 32.2 us
  matrix products: 18.5 us -> 0 us
  Pallas kernels: 0 us -> 9.72 us
    unnamed x5 -> x2, waiting for transfers between devices: 271 us -> 0.03 us
    all_gather x3 -> x1, waiting for transfers between devices: 214 us -> 0.02 us  [per_device(): w = lax.all_gather(halves(out_weight, c), 'y', axis=0, tiled=True)]
    select_n x128 -> x0, other arithmetic: 158 us -> none  [turn(): return jnp.where(reached, new, before)]
    all_to_all x0 -> x3, blocking collectives: none -> 41.7 us  [the longest x2 29.2 us: scan(): slices = lax.all_to_all(slices, ('z', 'x'), 0, 0)]
    ppermute x0 -> x3, starting transfers between devices: none -> 18.8 us  [swap(): return lax.ppermute(a, 'c', ((0, 1), (1, 0)))]
    dot_general x14 -> x0, matrix products: 18.5 us -> none  [the longest x1 3.1 us: per_device(): jnp.dot(tokens_dy, lax.all_gather(out_weight, 'dp', axis=0, tiled=True),...]
    all_to_all x0 -> x2, waiting for transfers between devices: none -> 15.3 us  [the longest x1 8.7 us: per_device(): lax.all_to_all(scattered.reshape(chips * 2, rows, half), ('z', 'x', 'c'),...]
    all_to_all x0 -> x2, starting transfers between devices: none -> 13.2 us  [the longest x1 9.39 us: per_device(): lax.all_to_all(scattered.reshape(chips * 2, rows, half), ('z', 'x', 'c'),...]
  transfers between devices with their start and end apart: 4 -> 7, of which waited for: 3 -> 2; matrix products, arithmetic and copies ran while one was open for 14% -> 5% of each run, Pallas kernels for 0% -> 7%
where the time goes in v1:
time: 132 us; the launch traced here: 131 us
  blocking collectives  41.7 us (32%)
  starting transfers between devices  32.2 us (24%)
  local copies, waits for them, and re-layouts  16.5 us (12%)
  waiting for transfers between devices  15.4 us (12%)
  between operations  14.3 us (11%)
  Pallas kernels  9.72 us (7%)
    all_to_all x2, blocking collectives, scan(): slices = lax.all_to_all(slices, ('z', 'x'), 0, 0)  29.2 us
    ppermute x3, starting transfers between devices, swap(): return lax.ppermute(a, 'c', ((0, 1), (1, 0)))  18.8 us
    all_to_all x1, blocking collectives, scan(): return lax.all_to_all(sums, ('z', 'x'), 0, 0).reshape(heads, HEAD, HEAD)  12.5 us
    unnamed x34, local copies, waits for them, and re-layouts  10.3 us
    pallas_call x8, Pallas kernels, call(): pl.pallas_call(kernel, grid_spec=pltpu.PrefetchScalarGridSpec(num_scalar_...  9.72 us
    all_to_all x1, starting transfers between devices, per_device(): lax.all_to_all(scattered.reshape(chips * 2, rows, half), ('z', 'x', 'c'),...  9.39 us
    all_to_all x1, waiting for transfers between devices, per_device(): lax.all_to_all(scattered.reshape(chips * 2, rows, half), ('z', 'x', 'c'),...  8.7 us
    all_to_all x1, waiting for transfers between devices, scan(): return lax.all_to_all(sums, ('z', 'x'), 0, 0).reshape(heads, HEAD, HEAD)  6.59 us
  transfers between devices with their start and end apart: 7, of which 2 were waited for; matrix products, arithmetic and copies ran while one was open for 5% of the time, Pallas kernels for 7%

profile of v1, /device:TPU:1, one launch (start us, length us, event | category | flops | bytes accessed | tf_op | source)
XLA Modules:
  0.0 130.7 jit_solution(12571281557707739852)
XLA Ops:
  7.2 0.0 copy-start
  7.2 0.0 all-gather.2.cloned.1.call-start
  7.2 0.9 copy-done
  8.1 0.7 constant_dynamic-slice_fusion
  8.8 0.0 all-gather.2.cloned.1.call-update
  8.8 0.0 copy-start.1
  8.8 1.1 constant_dynamic-slice_fusion.1
  9.9 0.0 copy-start.4
  10.0 0.1 pad_maximum_fusion.1
  10.0 0.0 copy-start.2
  10.0 0.0 copy-start.3
  10.0 8.9 %collective-permute-start.1 = (bf16[2,256,512]{2,1,0:T(8,128)(2,1)S(1)}, bf16[2,256,512]{2,1,0:T(8,128)(2,1)S(1)}, u32[]{:S(2)}, u32[]{:S(2)}) collective-permute-start(bf16[2,256,512]{2,1,0:T(8,128)(2,1)S(1)} %pad_maximum_fusion.1), channel_id=1, source_target_pairs={{0,1},{1,0},{2,3},{3,2},{4,5},{5,4},{6,7},{7,6},{8,9},{9,8},{10,11... | collective-permute-start | bytes 1572872 | tf_op jit(solution)/shard_map/ppermute | solution.py:163
  19.0 0.0 copy-done.1
  19.0 0.0 copy-done.4
  19.0 1.0 pad_maximum_fusion
  20.0 1.9 %collective-permute-start = (bf16[256,1536]{1,0:T(8,128)(2,1)}, bf16[256,1536]{1,0:T(8,128)(2,1)}, u32[]{:S(2)}, u32[]{:S(2)}) collective-permute-start(bf16[256,1536]{1,0:T(8,128)(2,1)} %pad_maximum_fusion), channel_id=1, source_target_pairs={{0,1},{1,0},{2,3},{3,2},{4,5},{5,4},{6,7},{7,6},{8,9},{9,8},{10,11... | collective-permute-start | bytes 2359304 | tf_op jit(solution)/shard_map/ppermute | solution.py:163
  21.9 0.0 collective-permute-done.1.kv_far
  21.9 0.0 copy-done.2
  21.9 0.0 copy-done.3
  21.9 0.4 shard_map.85
  22.3 0.0 copy-start.8
  22.3 0.7 copy-done.8
  23.0 0.0 copy-start.11
  23.0 0.7 copy-done.11
  23.7 16.6 %all_to_all.25.terms = bf16[32,16,128]{2,1,0:T(8,128)(2,1)S(1)} all-to-all(bf16[32,16,128]{2,1,0:T(8,128)(2,1)S(1)} %bitcast.30), channel_id=1, replica_groups=mesh['y'=8,'z'=8,'x'=4,'c'=2] {'z','x'}, dimensions={0} | all-to-all | bytes 262144 | tf_op jit(solution)/shard_map/all_to_all | solution.py:172
  40.4 0.7 shard_map.86
  41.0 3.8 %all-to-all-start.1 = ((bf16[32,16,128]{2,1,0:T(8,128)(2,1)}), bf16[32,16,128]{2,1,0:T(8,128)(2,1)S(1)}, u32[]{:S(2)}, u32[]{:S(2)}) async-start(bf16[32,16,128]{2,1,0:T(8,128)(2,1)} %shard_map.86), calls=%async_computation.1 | async-start | bytes 262144 | tf_op jit(solution)/shard_map/all_to_all | solution.py:174
  44.9 0.0 reduce-scatter.2.cloned.1.call-start
  45.0 0.0 collective-permute-done
  45.0 1.7 %slice.8.q_far = bf16[256,512]{1,0:T(8,128)(2,1)} slice(bf16[256,1536]{1,0:T(8,128)(2,1)} %collective-permute-done), slice={[0:256], [0:512]} | slice | bytes 524288 | tf_op jit(solution)/shard_map/slice | solution.py:168
  46.6 1.1 slice.9.dy_far
  47.7 6.6 %all-to-all-done.1 = bf16[32,16,128]{2,1,0:T(8,128)(2,1)S(1)} async-done(((bf16[32,16,128]{2,1,0:T(8,128)(2,1)}), bf16[32,16,128]{2,1,0:T(8,128)(2,1)S(1)}, u32[]{:S(2)}, u32[]{:S(2)}) %all-to-all-start.1) | async-done | bytes 131104 | tf_op jit(solution)/shard_map/all_to_all | solution.py:174
  54.3 0.9 copy-done.5
  55.3 0.0 copy-start.9
  55.3 0.9 copy-done.9
  56.2 0.0 copy-start.12
  56.2 0.9 copy-done.12
  57.2 2.0 %shard_map.90 = (bf16[1024,512]{1,0:T(8,128)(2,1)S(1)}, bf16[256,512]{1,0:T(8,128)(2,1)}, bf16[256,512]{1,0:T(8,128)(2,1)}) custom-call(s32[1]{0:T(128)} %bitcast.core, bf16[256,1024]{1,0:T(8,128)(2,1)S(1)} %bitcast.14, bf16[256,1024]{1,0:T(8,128)(2,1)S(1)} %bitcast.18, bf16[256,1024]{1,0:T(8,128)(2,1)S(1)} %bitcast.21, bf16[256,512]{1,0:T(8,128)(2,1)S(1)} %copy-done.5, ...), custom_call_target="tpu_custom_call" | custom-call | tf_op jit(solution)/shard_map/pallas_call | solution.py:32
  59.2 0.0 copy-start.14
  59.2 1.0 copy-done.14
  60.1 0.0 reduce-scatter.2.cloned.1.call-update
  60.2 0.0 all-gather.2.cloned.1.call-done.w
  60.2 0.0 copy-start.6
  60.2 0.9 copy-done.6
  61.1 0.0 copy-start.7
  61.1 1.2 copy-done.7
  62.4 0.0 copy-start.10
  62.4 1.0 shard_map.84
  63.4 12.5 %all_to_all.26.terms = bf16[32,16,128]{2,1,0:T(8,128)(2,1)S(1)} all-to-all(bf16[32,16,128]{2,1,0:T(8,128)(2,1)S(1)} %bitcast.29), channel_id=1, replica_groups=mesh['y'=8,'z'=8,'x'=4,'c'=2] {'z','x'}, dimensions={0} | all-to-all | bytes 262144 | tf_op jit(solution)/shard_map/all_to_all | solution.py:172
  76.0 12.5 %all_to_all.27 = bf16[32,16,128]{2,1,0:T(8,128)(2,1)S(1)} all-to-all(bf16[32,16,128]{2,1,0:T(8,128)(2,1)S(1)} %shard_map.87), channel_id=1, replica_groups=mesh['y'=8,'z'=8,'x'=4,'c'=2] {'z','x'}, dimensions={0} | all-to-all | bytes 262144 | tf_op jit(solution)/shard_map/all_to_all | solution.py:174
  88.5 0.0 copy-done.10
  88.5 0.0 copy-done.13
  88.5 3.7 %shard_map.88 = (bf16[3,256,512]{2,1,0:T(8,128)(2,1)S(1)}, bf16[3,256,512]{2,1,0:T(8,128)(2,1)}) custom-call(s32[1]{0:T(128)} %bitcast.core, bf16[256,1024]{1,0:T(8,128)(2,1)S(1)} %bitcast.16, bf16[256,1024]{1,0:T(8,128)(2,1)S(1)} %bitcast.19, bf16[256,1024]{1,0:T(8,128)(2,1)S(1)} %bitcast.22, bf16[256,512]{1,0:T(8,128)(2,1)S(1)} %copy-done.6, ...), custom_call_target="tpu_custom_call" | custom-call | tf_op jit(solution)/shard_map/pallas_call | solution.py:32
  92.2 0.9 copy-done.15
  93.1 8.0 %collective-permute-start.2 = (bf16[3,256,512]{2,1,0:T(8,128)(2,1)}, bf16[3,256,512]{2,1,0:T(8,128)(2,1)S(1)}, u32[]{:S(2)}, u32[]{:S(2)}) collective-permute-start(bf16[3,256,512]{2,1,0:T(8,128)(2,1)} %get-tuple-element.27), channel_id=1, source_target_pairs={{0,1},{1,0},{2,3},{3,2},{4,5},{5,4},{6,7},{7,6},{8,9},{9,8},{10,11... | collective-permute-start | bytes 2359304 | tf_op jit(solution)/shard_map/ppermute | solution.py:163
  101.1 0.0 reduce-scatter.2.cloned.1.call-done
  101.1 1.6 %reshape.36 = bf16[64,2,512]{2,1,0:T(2,128)(2,1)} reshape(bf16[128,512]{1,0:T(8,128)(2,1)} %reduce-scatter.2.cloned.1.call-done) | data formatting | bytes 262144 | tf_op jit(solution)/shard_map/reshape | solution.py:205
  102.8 9.4 %all-to-all-start.4 = ((bf16[64,2,512]{2,1,0:T(2,128)(2,1)}), bf16[64,2,512]{2,1,0:T(2,128)(2,1)S(1)}, u32[]{:S(2)}, u32[]{:S(2)}) async-start(bf16[64,2,512]{2,1,0:T(2,128)(2,1)} %reshape.36), calls=%async_computation.5 | async-start | bytes 262144 | tf_op jit(solution)/shard_map/all_to_all | solution.py:205
  112.2 0.0 collective-permute-done.2.far
  112.2 0.0 copy-start.16
  112.2 1.1 copy-done.16
  113.3 1.3 shard_map.89
  114.6 8.7 %all-to-all-done.4.parts = bf16[64,2,512]{2,1,0:T(2,128)(2,1)S(1)} async-done(((bf16[64,2,512]{2,1,0:T(2,128)(2,1)}), bf16[64,2,512]{2,1,0:T(2,128)(2,1)S(1)}, u32[]{:S(2)}, u32[]{:S(2)}) %all-to-all-start.4) | async-done | bytes 131104 | tf_op jit(solution)/shard_map/all_to_all | solution.py:205
  123.3 0.6 shard_map.91
  (5 shorter events, 0.1 us)
Async XLA Ops:
  7.2 1.0 copy-start
  7.2 53.0 %all-gather.2.cloned.1.call-start = ((), (), s32[]{:S(2)}) async-start(), calls=%async_computation.6 | async-start | bytes 1179648 | tf_op jit(solution)/shard_map/all_gather | solution.py:165
  8.8 10.2 %copy-start.1 = (bf16[1,256,1024]{2,1,0:T(8,128)(2,1)S(1)}, bf16[1,256,1024]{2,1,0:T(8,128)(2,1)}, u32[]{:S(2)}) copy-start(bf16[1,256,1024]{2,1,0:T(8,128)(2,1)} %param.5) | copy-start | bytes 1572868
  9.9 9.1 %copy-start.4 = (bf16[1,256,1024]{2,1,0:T(8,128)(2,1)S(1)}, bf16[1,256,1024]{2,1,0:T(8,128)(2,1)}, u32[]{:S(2)}) copy-start(bf16[1,256,1024]{2,1,0:T(8,128)(2,1)} %param.8) | copy-start | bytes 1572868
  10.0 11.9 %copy-start.2 = (bf16[1,256,1024]{2,1,0:T(8,128)(2,1)S(1)}, bf16[1,256,1024]{2,1,0:T(8,128)(2,1)}, u32[]{:S(2)}) copy-start(bf16[1,256,1024]{2,1,0:T(8,128)(2,1)} %param.6) | copy-start | bytes 1572868
  10.0 11.9 %copy-start.3 = (bf16[1,256,1024]{2,1,0:T(8,128)(2,1)S(1)}, bf16[1,256,1024]{2,1,0:T(8,128)(2,1)}, u32[]{:S(2)}) copy-start(bf16[1,256,1024]{2,1,0:T(8,128)(2,1)} %param.7) | copy-start | bytes 1572868
  10.0 11.9 %collective-permute-start.1 = (bf16[2,256,512]{2,1,0:T(8,128)(2,1)S(1)}, bf16[2,256,512]{2,1,0:T(8,128)(2,1)S(1)}, u32[]{:S(2)}, u32[]{:S(2)}) collective-permute-start(bf16[2,256,512]{2,1,0:T(8,128)(2,1)S(1)} %pad_maximum_fusion.1), channel_id=1, source_target_pairs={{0,1},{1,0},{2,3},{3,2},{4,5},{5,4},{6,7},{7,6},{8,9},{9,8},{10,11... | collective-permute-start | bytes 1572872 | tf_op jit(solution)/shard_map/ppermute | solution.py:163
  20.0 25.0 %collective-permute-start = (bf16[256,1536]{1,0:T(8,128)(2,1)}, bf16[256,1536]{1,0:T(8,128)(2,1)}, u32[]{:S(2)}, u32[]{:S(2)}) collective-permute-start(bf16[256,1536]{1,0:T(8,128)(2,1)} %pad_maximum_fusion), channel_id=1, source_target_pairs={{0,1},{1,0},{2,3},{3,2},{4,5},{5,4},{6,7},{7,6},{8,9},{9,8},{10,11... | collective-permute-start | bytes 2359304 | tf_op jit(solution)/shard_map/ppermute | solution.py:163
  22.3 0.7 copy-start.8
  23.0 0.7 copy-start.11
  41.0 13.3 %all-to-all-start.1 = ((bf16[32,16,128]{2,1,0:T(8,128)(2,1)}), bf16[32,16,128]{2,1,0:T(8,128)(2,1)S(1)}, u32[]{:S(2)}, u32[]{:S(2)}) async-start(bf16[32,16,128]{2,1,0:T(8,128)(2,1)} %shard_map.86), calls=%async_computation.1 | async-start | bytes 262144 | tf_op jit(solution)/shard_map/all_to_all | solution.py:174
  44.9 56.2 %reduce-scatter.2.cloned.1.call-start = ((), (), s32[]{:S(2)}) async-start(), calls=%async_computation.7 | async-start | bytes 1179648 | tf_op jit(solution)/shard_map/reduce_scatter | solution.py:187
  54.3 1.0 copy-start.5
  55.3 0.9 copy-start.9
  56.2 0.9 copy-start.12
  59.2 1.0 copy-start.14
  60.2 1.0 copy-start.6
  61.1 1.2 copy-start.7
  62.4 26.1 %copy-start.10 = (f32[4,128,128]{2,1,0:T(8,128)S(1)}, f32[4,128,128]{2,1,0:T(8,128)}, u32[]{:S(2)}) copy-start(f32[4,128,128]{2,1,0:T(8,128)} %copy-done.8) | copy-start | bytes 786436
  62.4 26.1 %copy-start.13 = (f32[4,128,128]{2,1,0:T(8,128)S(1)}, f32[4,128,128]{2,1,0:T(8,128)}, u32[]{:S(2)}) copy-start(f32[4,128,128]{2,1,0:T(8,128)} %copy-done.11) | copy-start | bytes 786436
  92.2 0.9 copy-start.15
  93.1 19.1 %collective-permute-start.2 = (bf16[3,256,512]{2,1,0:T(8,128)(2,1)}, bf16[3,256,512]{2,1,0:T(8,128)(2,1)S(1)}, u32[]{:S(2)}, u32[]{:S(2)}) collective-permute-start(bf16[3,256,512]{2,1,0:T(8,128)(2,1)} %get-tuple-element.27), channel_id=1, source_target_pairs={{0,1},{1,0},{2,3},{3,2},{4,5},{5,4},{6,7},{7,6},{8,9},{9,8},{10,11... | collective-permute-start | bytes 2359304 | tf_op jit(solution)/shard_map/ppermute | solution.py:163
  102.8 20.5 %all-to-all-start.4 = ((bf16[64,2,512]{2,1,0:T(2,128)(2,1)}), bf16[64,2,512]{2,1,0:T(2,128)(2,1)S(1)}, u32[]{:S(2)}, u32[]{:S(2)}) async-start(bf16[64,2,512]{2,1,0:T(2,128)(2,1)} %reshape.36), calls=%async_computation.5 | async-start | bytes 262144 | tf_op jit(solution)/shard_map/all_to_all | solution.py:205
  112.2 1.1 copy-start.16
Sparse Core Ops, SparseCore 0:
  10.1 42.3 all-gather.1
  60.3 34.8 reduce-scatter.1

commit v2 on v1

v2 whole, which is shorter than its diff:
```python
import functools
import math

import jax
import jax.numpy as jnp
from jax import lax
from jax.experimental import pallas as pl
from jax.experimental.pallas import tpu as pltpu
from jax.sharding import Mesh, PartitionSpec as P

HEAD = 128
F32 = jnp.float32
BF16 = jnp.bfloat16


def dot(a, b, contract):
    return lax.dot_general(a, b, ((contract[:1], contract[1:]), ((), ())), preferred_element_type=F32)


def head(ref, h):
    return ref[:, h * HEAD : (h + 1) * HEAD]


def call(kernel, core, ins, outs, scratch=(), vmem=60):
    def spec(operand):
        if isinstance(operand, tuple):
            array, columns, place = operand
            if place is None:
                return pl.BlockSpec((array.shape[0], columns), lambda i, c: (0, c[0]))
            return pl.BlockSpec((array.shape[0], columns), lambda i, c: (0, place))
        return pl.BlockSpec(operand.shape, lambda i, c, n=operand.ndim: (0,) * n)

    arrays = [operand[0] if isinstance(operand, tuple) else operand for operand in ins]
    return pl.pallas_call(
        kernel,
        grid_spec=pltpu.PrefetchScalarGridSpec(
            num_scalar_prefetch=1,
            grid=(1,),
            in_specs=[spec(operand) for operand in ins],
            out_specs=[pl.BlockSpec(o.shape, lambda i, c, n=len(o.shape): (0,) * n) for o in outs],
            scratch_shapes=scratch,
        ),
        out_shape=outs,
        compiler_params=pltpu.CompilerParams(vmem_limit_bytes=vmem * 1024 * 1024),
    )(core, *arrays)


def shape(dims, dtype):
    return jax.ShapeDtypeStruct(dims, dtype)


def masked(scores, factor):
    rows = lax.broadcasted_iota(jnp.int32, scores.shape, 0)
    columns = lax.broadcasted_iota(jnp.int32, scores.shape, 1)
    return jnp.where(rows >= columns, factor * scores, 0.0).astype(BF16)


def entering(chunk, inside, here):
    return (chunk.astype(F32) + jnp.where(here, inside, 0.0)).astype(BF16)


def local_kernel(factor, core, q, k, v, dy, far, near_state, far_state, near_out, far_out, dy_turned):
    half = q.shape[1]
    tokens = q.shape[0]
    q_far, k_far, v_far = (far.at[:, i * half : (i + 1) * half] for i in range(3))
    for h in range(near_state.shape[0]):
        at = slice(h * HEAD, (h + 1) * HEAD)
        for qs, ks, vs, state, o in ((q, k, v, near_state, near_out), (q_far, k_far, v_far, far_state, far_out)):
            qh, kh, vh = head(qs, h), head(ks, h), head(vs, h)
            state[h] = dot(kh, vh, (0, 0))
            o[:, at] = dot(masked(dot(qh, kh, (1, 1)), factor), vh, (1, 0))
    dy_turned[:, :tokens] = dy[...].T
    dy_turned[:, tokens:] = far[:, 3 * half :].T


def d_out_kernel(core, dy, far, w, q, near_state, far_state, d, d_far, near, other, both):
    half = q.shape[1]
    d[...] = dot(dy[...], w[...], (1, 0)).astype(BF16)
    d_far[...] = dot(far[:, 3 * half :], w[...], (1, 0)).astype(BF16)
    chips, lines, _ = both.shape
    lines = lines // 2
    per_head = HEAD // lines
    for h in range(near.shape[0]):
        g = dot(head(q, h), head(d, h), (0, 0))
        g_far = dot(head(far, h), head(d_far, h), (0, 0))
        near[h] = g
        other[h] = g_far
        for side, total in ((0, near_state[h] + far_state[h]), (1, g + g_far)):
            total = total.astype(BF16).reshape(per_head, lines, HEAD)
            both[h * per_head : (h + 1) * per_head, side * lines : (side + 1) * lines, :] = total


def prefix_kernel(core, terms, sums):
    count, lines, _ = terms.shape
    half = lines // 2
    for order, at in ((range(count), slice(0, half)), (reversed(range(count)), slice(half, lines))):
        total = jnp.zeros((half, HEAD), F32)
        for k in order:
            sums[k, at, :] = total.astype(BF16)
            total = total + terms[k, at, :].astype(F32)


def chunk_sum(sums, h, side):
    _, lines, _ = sums.shape
    lines = lines // 2
    per_head = HEAD // lines
    return sums[h * per_head : (h + 1) * per_head, side * lines : (side + 1) * lines, :].reshape(HEAD, HEAD)


def output_kernel(factor, core, q, far, sums, s_near, s_far, local, local_far, dy_turned, weight, out, held):
    tokens = q.shape[0]
    for h in range(s_near.shape[0]):
        at = slice(h * HEAD, (h + 1) * HEAD)
        prior = chunk_sum(sums, h, 0)
        for qs, inside, here, part, rows in (
            (q, s_far, core[0] == 1, local, slice(0, tokens)),
            (far, s_near, core[0] == 0, local_far, slice(tokens, 2 * tokens)),
        ):
            before = entering(prior, inside[h], here)
            out[rows, at] = (part[:, at] + factor * dot(head(qs, h), before, (1, 0))).astype(BF16)
    whole = dot(dy_turned[...], out[...], (1, 0))
    for b in range(s_near.shape[0]):
        held[b] = whole[:, b * HEAD : (b + 1) * HEAD]
    places, lines, count, _ = weight.shape
    for x in range(places):
        for t in range(lines):
            for b in range(s_near.shape[0]):
                at = slice(b * HEAD, (b + 1) * HEAD)
                weight[x, t, :, at] = held[b, pl.ds(x * lines + t, count, stride=places * lines), :].astype(BF16)


def grads_kernel(factor, core, q, k, v, far, d, d_far, sums, s_near, s_far, g_near, g_far, near, other):
    first = core[0] == 0
    half = q.shape[1]
    q_far, k_far, v_far = (far.at[:, i * half : (i + 1) * half] for i in range(3))
    for h in range(s_near.shape[0]):
        at = slice(h * HEAD, (h + 1) * HEAD)
        prior, later = chunk_sum(sums, h, 0), chunk_sum(sums, h, 1)
        for qs, ks, vs, ds, s_in, s_here, g_in, g_here, o in (
            (q, k, v, d, s_far, core[0] == 1, g_far, first, near),
            (q_far, k_far, v_far, d_far, s_near, first, g_near, core[0] == 1, other),
        ):
            qh, kh, vh, dh = head(qs, h), head(ks, h), head(vs, h), head(ds, h)
            before = entering(prior, s_in[h], s_here)
            after = entering(later, g_in[h], g_here)
            scores = masked(dot(qh, kh, (1, 1)), factor)
            score_grad = masked(dot(dh, vh, (1, 1)), factor)
            o[0, :, at] = (dot(score_grad, kh, (1, 0)) + factor * dot(dh, before, (1, 1))).astype(BF16)
            o[1, :, at] = (dot(score_grad, qh, (0, 0)) + factor * dot(vh, after, (1, 1))).astype(BF16)
            o[2, :, at] = (dot(scores, dh, (0, 0)) + factor * dot(kh, after, (1, 0))).astype(BF16)


def join_kernel(core, near, far, q_grad, k_grad, v_grad):
    width = near.shape[2]
    for i, o in enumerate((q_grad, k_grad, v_grad)):

        @pl.when(core[0] == 0)
        def _():
            o[:, :width] = near[i]
            o[:, width:] = far[i]

        @pl.when(core[0] == 1)
        def _():
            o[:, :width] = far[i]
            o[:, width:] = near[i]


def gather_rows_kernel(core, parts, lines, held):
    places, rows, count, columns = parts.shape
    blocks = columns // HEAD
    for t in range(rows):
        for b in range(blocks):
            total = jnp.zeros((count, HEAD), F32)
            for x in range(places):
                total = total + parts[x, t, :, b * HEAD : (b + 1) * HEAD].astype(F32)
            held[pl.ds(t * blocks + b, count, stride=rows * blocks), :] = total
    lines[...] = held[...].astype(BF16)


def sum_kernel(scale, core, parts, total, held):
    count, lines, _ = parts.shape
    rows, width = total.shape
    blocks = lines // rows
    for side in range(2):
        added = jnp.zeros((lines, HEAD), F32)
        for k in range(side, count, 2):
            added = added + parts[k].astype(F32)
        held[...] = added * scale
        for b in range(blocks):
            at = side * blocks * HEAD + b * HEAD
            total[:, at : at + HEAD] = held[pl.ds(b, rows, stride=blocks), :]


def per_device(query, keys, values, cotangent, out_weight):
    q, k, v, dy = query[0], keys[0], values[0], cotangent[0]
    stretch, width = q.shape
    half = width // 2
    heads = half // HEAD
    sizes = {axis: lax.axis_size(axis) for axis in ("y", "z", "x", "c")}
    chips = sizes["z"] * sizes["x"]
    seq_len = stretch * chips * 2
    factor = 1.0 / math.sqrt(HEAD * seq_len)
    grad_factor = 1.0 / math.sqrt(sizes["y"] * seq_len)
    c = lax.axis_index("c")
    core = c.reshape(1).astype(jnp.int32)

    def halves(a, index):
        return lax.dynamic_slice_in_dim(a, index * half, half, 1)

    def swap(a):
        return lax.ppermute(a, "c", ((0, 1), (1, 0)))

    copies = jnp.broadcast_to(halves(out_weight, c)[None], (sizes["y"], width // sizes["y"], half))
    w = lax.all_to_all(copies, "y", 0, 0).reshape(width, half)
    far = swap(jnp.concatenate([halves(q, 1 - c), halves(k, 1 - c), halves(v, 1 - c), dy], 1))
    own = [(a, half, None) for a in (q, k, v)]

    state = shape((heads, HEAD, HEAD), F32)
    tokens = shape((stretch, half), BF16)
    part = shape((stretch, half), F32)
    s_near, s_far, local, local_far, dy_turned = call(
        functools.partial(local_kernel, factor),
        core,
        own + [dy, far],
        [state, state, part, part, shape((width, 2 * stretch), BF16)],
    )
    slices = shape((chips, 2 * heads * HEAD // chips, HEAD), BF16)
    d, d_far, g_near, g_far, both = call(
        d_out_kernel, core, [dy, far, w, own[0], s_near, s_far], [tokens, tokens, state, state, slices]
    )
    both = lax.all_to_all(both, ("z", "x"), 0, 0)
    (sums,) = call(prefix_kernel, core, [both], [slices])
    sums = lax.all_to_all(sums, ("z", "x"), 0, 0)

    rows = width // sizes["y"] // (chips * 2)
    blocks = half // HEAD
    places = sizes["y"] * sizes["z"]
    partial, _ = call(
        functools.partial(output_kernel, factor),
        core,
        [own[0], far, sums, s_near, s_far, local, local_far, dy_turned],
        [shape((sizes["x"], 2 * rows, places, half), BF16), shape((2 * stretch, half), BF16)],
        [pltpu.VMEM((blocks, width, HEAD), F32)],
    )
    parts = lax.all_to_all(partial, "x", 0, 0)

    grads = shape((3, stretch, half), BF16)
    near, other = call(
        functools.partial(grads_kernel, factor),
        core,
        own + [far, d, d_far, sums, s_near, s_far, g_near, g_far],
        [grads, grads],
    )
    back = swap(other)
    whole = shape((stretch, width), BF16)
    q_grad, k_grad, v_grad = call(join_kernel, core, [near, back], [whole] * 3)

    lines = shape((places * 2 * rows * blocks, HEAD), BF16)
    (summed,) = call(gather_rows_kernel, core, [parts], [lines], [pltpu.VMEM(lines.shape, F32)])
    summed = lax.all_to_all(summed.reshape(places * 2, rows * blocks, HEAD), ("y", "z", "c"), 0, 0)
    (weight_grad,) = call(
        functools.partial(sum_kernel, grad_factor),
        core,
        [summed],
        [shape((rows, width), F32)],
        [pltpu.VMEM((rows * blocks, HEAD), F32)],
    )
    return q_grad[None], k_grad[None], v_grad[None], weight_grad


def solution(mesh):
    dp, ctx = mesh.devices.shape
    chips = Mesh(mesh.devices.reshape(dp, ctx // 8, 4, 2), ("y", "z", "x", "c"))
    tokens = P("y", ("z", "x", "c"), None)
    return jax.shard_map(
        per_device,
        mesh=chips,
        in_specs=(tokens, tokens, tokens, tokens, P("y", None)),
        out_specs=(tokens, tokens, tokens, P(("y", "z", "x", "c"), None)),
        check_vma=False,
    )
```

time: 132 us -> 135 us (1.023)
  Pallas kernels: 9.72 us -> 27.1 us
  between operations: 14.3 us -> 0.77 us
  waiting for transfers between devices: 15.4 us -> 25.3 us
  local copies, waits for them, and re-layouts: 16.5 us -> 6.67 us
    pallas_call x8, Pallas kernels: 9.72 us -> 27.1 us  [call(): pl.pallas_call(kernel, grid_spec=pltpu.PrefetchScalarGridSpec(num_scalar_...]
    all_to_all x2 -> x3, starting transfers between devices: 13.2 us -> 21.1 us  [the longest x1 9.77 us: per_device(): lax.all_to_all(summed.reshape(places * 2, rows * blocks, HEAD), ('y', 'z'...]
    ppermute x3 -> x2, starting transfers between devices: 18.8 us -> 11.1 us  [swap(): return lax.ppermute(a, 'c', ((0, 1), (1, 0)))]
    all_to_all x2 -> x3, waiting for transfers between devices: 15.3 us -> 22.7 us  [the longest x1 11.9 us: per_device(): w = lax.all_to_all(copies, 'y', 0, 0).reshape(width, half)]
    unnamed x34 -> x18, local copies, waits for them, and re-layouts: 10.3 us -> 5.52 us
    slice x2 -> x0, local copies, waits for them, and re-layouts: 2.75 us -> none  [per_device(): q_far, dy_far = (q_dy_far[:, :half], q_dy_far[:, half:])]
    ppermute x3 -> x2, waiting for transfers between devices: 0.01 us -> 2.64 us  [swap(): return lax.ppermute(a, 'c', ((0, 1), (1, 0)))]
    dynamic_slice x3, local copies, waits for them, and re-layouts: 1.81 us -> 0.08 us  [halves(): return lax.dynamic_slice_in_dim(a, index * half, half, 1)]
  transfers between devices with their start and end apart: 7 -> 5, of which waited for: 2 -> 3; matrix products, arithmetic and copies ran while one was open for 5% -> 0% of each run, Pallas kernels for 7% -> 11%
where the time goes in v2:
time: 135 us; the launch traced here: 134 us
  blocking collectives  42.1 us (31%)
  starting transfers between devices  32.1 us (24%)
  Pallas kernels  27.1 us (20%)
  waiting for transfers between devices  25.3 us (19%)
  local copies, waits for them, and re-layouts  6.67 us (5%)
    pallas_call x8, Pallas kernels, call(): pl.pallas_call(kernel, grid_spec=pltpu.PrefetchScalarGridSpec(num_scalar_...  27.1 us
    all_to_all x1, blocking collectives, per_device(): both = lax.all_to_all(both, ('z', 'x'), 0, 0)  27.1 us
    all_to_all x1, blocking collectives, per_device(): sums = lax.all_to_all(sums, ('z', 'x'), 0, 0)  15.1 us
    all_to_all x1, waiting for transfers between devices, per_device(): w = lax.all_to_all(copies, 'y', 0, 0).reshape(width, half)  11.9 us
    ppermute x2, starting transfers between devices, swap(): return lax.ppermute(a, 'c', ((0, 1), (1, 0)))  11.1 us
    all_to_all x1, waiting for transfers between devices, per_device(): lax.all_to_all(summed.reshape(places * 2, rows * blocks, HEAD), ('y', 'z'...  10.8 us
    all_to_all x1, starting transfers between devices, per_device(): lax.all_to_all(summed.reshape(places * 2, rows * blocks, HEAD), ('y', 'z'...  9.77 us
    all_to_all x1, starting transfers between devices, per_device(): w = lax.all_to_all(copies, 'y', 0, 0).reshape(width, half)  7.78 us
  transfers between devices with their start and end apart: 5, of which 3 were waited for; matrix products, arithmetic and copies ran while one was open for 0% of the time, Pallas kernels for 11%

profile of v2, /device:TPU:1, one launch (start us, length us, event | category | flops | bytes accessed | tf_op | source)
XLA Modules:
  0.0 134.2 jit_solution(14743194725082589184)
XLA Ops:
  0.6 0.0 copy-start
  0.7 0.9 copy-done
  1.6 1.1 broadcast_in_dim.15
  2.7 0.0 copy-start.2
  2.7 0.0 copy-start.5
  2.7 0.0 copy-start.6
  2.7 7.8 %all-to-all-start = ((bf16[8,128,512]{2,1,0:T(8,128)(2,1)}), bf16[8,128,512]{2,1,0:T(8,128)(2,1)}, u32[]{:S(2)}, u32[]{:S(2)}) async-start(bf16[8,128,512]{2,1,0:T(8,128)(2,1)} %broadcast_in_dim.15), calls=%async_computation | async-start | bytes 2097152 | tf_op jit(solution)/shard_map/all_to_all | solution.py:214
  10.5 0.0 copy-start.3
  10.5 0.0 copy-done.2
  10.5 0.0 copy-done.5
  10.5 0.0 copy-done.6
  10.6 0.9 copy-done.3
  11.5 0.1 pad_maximum_fusion
  11.6 5.4 %collective-permute-start = (bf16[256,2560]{1,0:T(8,128)(2,1)S(1)}, bf16[256,2560]{1,0:T(8,128)(2,1)S(1)}, u32[]{:S(2)}, u32[]{:S(2)}) collective-permute-start(bf16[256,2560]{1,0:T(8,128)(2,1)S(1)} %pad_maximum_fusion), channel_id=1, source_target_pairs={{0,1},{1,0},{2,3},{3,2},{4,5},{5,4},{6,7},{7,6},{8,9},{9,8},{10,11... | collective-permute-start | bytes 3932168 | tf_op jit(solution)/shard_map/ppermute | solution.py:211
  17.0 2.6 %collective-permute-done.far = bf16[256,2560]{1,0:T(8,128)(2,1)S(1)} collective-permute-done((bf16[256,2560]{1,0:T(8,128)(2,1)S(1)}, bf16[256,2560]{1,0:T(8,128)(2,1)S(1)}, u32[]{:S(2)}, u32[]{:S(2)}) %collective-permute-start) | collective-permute-done | bytes 1310752 | tf_op jit(solution)/shard_map/ppermute | solution.py:211
  19.6 0.0 copy-start.1
  19.6 1.1 copy-done.1
  20.7 4.6 %shard_map.84 = (f32[4,128,128]{2,1,0:T(8,128)}, f32[4,128,128]{2,1,0:T(8,128)}, f32[256,512]{1,0:T(8,128)}, f32[256,512]{1,0:T(8,128)}, bf16[1024,512]{1,0:T(8,128)(2,1)}) custom-call(s32[1]{0:T(128)} %bitcast.core, bf16[256,1024]{1,0:T(8,128)(2,1)} %bitcast.16, bf16[256,1024]{1,0:T(8,128)(2,1)} %bitcast.23, bf16[256,1024]{1,0:T(8,128)(2,1)} %bitcast.25, ...), custom_call_target="tpu_custom_call" | custom-call | tf_op jit(solution)/shard_map/pallas_call | solution.py:34
  25.3 11.9 %all-to-all-done = bf16[8,128,512]{2,1,0:T(8,128)(2,1)} async-done(((bf16[8,128,512]{2,1,0:T(8,128)(2,1)}), bf16[8,128,512]{2,1,0:T(8,128)(2,1)}, u32[]{:S(2)}, u32[]{:S(2)}) %all-to-all-start) | async-done | bytes 1048608 | tf_op jit(solution)/shard_map/all_to_all | solution.py:214
  37.2 3.8 %shard_map.85 = (bf16[256,512]{1,0:T(8,128)(2,1)}, bf16[256,512]{1,0:T(8,128)(2,1)}, f32[4,128,128]{2,1,0:T(8,128)}, f32[4,128,128]{2,1,0:T(8,128)}, bf16[32,32,128]{2,1,0:T(8,128)(2,1)}) custom-call(s32[1]{0:T(128)} %bitcast.core, bf16[256,1024]{1,0:T(8,128)(2,1)} %bitcast.21, bf16[256,2560]{1,0:T(8,128)(2,1)} %copy-done.1, bf16[1024,512]{1,0:T(8,128)(2,1)} %bitcast.8.w, ...), custom_call_target="tpu_custom_call" | custom-call | tf_op jit(solution)/shard_map/pallas_call | solution.py:34
  40.9 27.1 %all_to_all.25.terms = bf16[32,32,128]{2,1,0:T(8,128)(2,1)} all-to-all(bf16[32,32,128]{2,1,0:T(8,128)(2,1)} %get-tuple-element.24), channel_id=1, replica_groups=mesh['y'=8,'z'=8,'x'=4,'c'=2] {'z','x'}, dimensions={0} | all-to-all | bytes 524288 | tf_op jit(solution)/shard_map/all_to_all | solution.py:231
  68.0 1.7 %shard_map.86 = bf16[32,32,128]{2,1,0:T(8,128)(2,1)} custom-call(s32[1]{0:T(128)} %bitcast.core, bf16[32,32,128]{2,1,0:T(8,128)(2,1)} %all_to_all.25.terms), custom_call_target="tpu_custom_call" | custom-call | tf_op jit(solution)/shard_map/pallas_call | solution.py:34
  69.7 15.1 %all_to_all.26.sums = bf16[32,32,128]{2,1,0:T(8,128)(2,1)} all-to-all(bf16[32,32,128]{2,1,0:T(8,128)(2,1)} %shard_map.86), channel_id=1, replica_groups=mesh['y'=8,'z'=8,'x'=4,'c'=2] {'z','x'}, dimensions={0} | all-to-all | bytes 524288 | tf_op jit(solution)/shard_map/all_to_all | solution.py:233
  84.8 4.8 %shard_map.89 = (bf16[4,4,64,512]{3,2,1,0:T(8,128)(2,1)}, bf16[512,512]{1,0:T(8,128)(2,1)}) custom-call(s32[1]{0:T(128)} %bitcast.core, bf16[256,1024]{1,0:T(8,128)(2,1)} %bitcast.18, bf16[256,2560]{1,0:T(8,128)(2,1)} %copy-done.1, bf16[32,32,128]{2,1,0:T(8,128)(2,1)} %all_to_all.26.sums, f32[4,128,128]{2,1,0:T(8,128)} %get-tuple-element.20.near_state.s_near, ...), custom_call_target="tpu_custom_call" | custom-call | tf_op jit(solution)/shard_map/pallas_call | solution.py:34
  89.6 3.5 %all-to-all-start.3 = ((bf16[4,4,64,512]{3,2,1,0:T(8,128)(2,1)}), bf16[4,4,64,512]{3,2,1,0:T(8,128)(2,1)S(1)}, u32[]{:S(2)}, u32[]{:S(2)}) async-start(bf16[4,4,64,512]{3,2,1,0:T(8,128)(2,1)} %get-tuple-element.35), calls=%async_computation.3 | async-start | bytes 2097152 | tf_op jit(solution)/shard_map/all_to_all | solution.py:245
  93.1 5.7 %shard_map.87 = (bf16[3,256,512]{2,1,0:T(8,128)(2,1)}, bf16[3,256,512]{2,1,0:T(8,128)(2,1)}) custom-call(s32[1]{0:T(128)} %bitcast.core, bf16[256,1024]{1,0:T(8,128)(2,1)} %bitcast.19, bf16[256,1024]{1,0:T(8,128)(2,1)} %bitcast.24, bf16[256,1024]{1,0:T(8,128)(2,1)} %bitcast.26, bf16[256,2560]{1,0:T(8,128)(2,1)} %copy-done.1, ...), custom_call_target="tpu_custom_call" | custom-call | tf_op jit(solution)/shard_map/pallas_call | solution.py:34
  98.8 5.7 %collective-permute-start.1 = (bf16[3,256,512]{2,1,0:T(8,128)(2,1)}, bf16[3,256,512]{2,1,0:T(8,128)(2,1)S(1)}, u32[]{:S(2)}, u32[]{:S(2)}) collective-permute-start(bf16[3,256,512]{2,1,0:T(8,128)(2,1)} %get-tuple-element.28), channel_id=1, source_target_pairs={{0,1},{1,0},{2,3},{3,2},{4,5},{5,4},{6,7},{7,6},{8,9},{9,8},{10,11... | collective-permute-start | bytes 2359304 | tf_op jit(solution)/shard_map/ppermute | solution.py:211
  104.5 0.0 all-to-all-done.3.parts
  104.5 0.0 copy-start.4
  104.5 1.0 copy-done.4
  105.5 2.2 %shard_map.90 = bf16[1024,128]{1,0:T(8,128)(2,1)} custom-call(s32[1]{0:T(128)} %bitcast.core, bf16[4,4,64,512]{3,2,1,0:T(8,128)(2,1)} %copy-done.4), custom_call_target="tpu_custom_call" | custom-call | tf_op jit(solution)/shard_map/pallas_call | solution.py:34
  107.7 9.8 %all-to-all-start.4 = ((bf16[128,8,128]{2,1,0:T(8,128)(2,1)}), bf16[128,8,128]{2,1,0:T(8,128)(2,1)S(1)}, u32[]{:S(2)}, u32[]{:S(2)}) async-start(bf16[128,8,128]{2,1,0:T(8,128)(2,1)} %bitcast.27), calls=%async_computation.4 | async-start | bytes 524288 | tf_op jit(solution)/shard_map/all_to_all | solution.py:260
  117.5 0.0 collective-permute-done.1.far
  117.5 0.0 copy-start.8
  117.5 0.9 copy-done.8
  118.4 2.6 %shard_map.88 = (bf16[256,1024]{1,0:T(8,128)(2,1)}, bf16[256,1024]{1,0:T(8,128)(2,1)}, bf16[256,1024]{1,0:T(8,128)(2,1)}) custom-call(s32[1]{0:T(128)} %bitcast.core, bf16[3,256,512]{2,1,0:T(8,128)(2,1)} %get-tuple-element.27.near, bf16[3,256,512]{2,1,0:T(8,128)(2,1)} %copy-done.8), custom_call_target="tpu_custom_call" | custom-call | tf_op jit(solution)/shard_map/pallas_call | solution.py:34
  121.0 10.8 %all-to-all-done.4.parts = bf16[128,8,128]{2,1,0:T(8,128)(2,1)S(1)} async-done(((bf16[128,8,128]{2,1,0:T(8,128)(2,1)}), bf16[128,8,128]{2,1,0:T(8,128)(2,1)S(1)}, u32[]{:S(2)}, u32[]{:S(2)}) %all-to-all-start.4) | async-done | bytes 262176 | tf_op jit(solution)/shard_map/all_to_all | solution.py:260
  131.9 0.0 copy-start.7
  131.9 0.7 copy-done.7
  132.6 1.6 %shard_map.91 = f32[2,1024]{1,0:T(2,128)} custom-call(s32[1]{0:T(128)} %bitcast.core, bf16[128,8,128]{2,1,0:T(8,128)(2,1)} %copy-done.7), custom_call_target="tpu_custom_call" | custom-call | tf_op jit(solution)/shard_map/pallas_call | solution.py:34
  (3 shorter events, 0.1 us)
Async XLA Ops:
  0.6 1.0 copy-start
  2.7 7.8 %copy-start.2 = (bf16[1,256,1024]{2,1,0:T(8,128)(2,1)S(1)}, bf16[1,256,1024]{2,1,0:T(8,128)(2,1)}, u32[]{:S(2)}) copy-start(bf16[1,256,1024]{2,1,0:T(8,128)(2,1)} %param.5) | copy-start | bytes 1572868
  2.7 7.8 %copy-start.5 = (bf16[1,256,1024]{2,1,0:T(8,128)(2,1)S(1)}, bf16[1,256,1024]{2,1,0:T(8,128)(2,1)}, u32[]{:S(2)}) copy-start(bf16[1,256,1024]{2,1,0:T(8,128)(2,1)} %param.6) | copy-start | bytes 1572868
  2.7 7.9 %copy-start.6 = (bf16[1,256,1024]{2,1,0:T(8,128)(2,1)S(1)}, bf16[1,256,1024]{2,1,0:T(8,128)(2,1)}, u32[]{:S(2)}) copy-start(bf16[1,256,1024]{2,1,0:T(8,128)(2,1)} %param.7) | copy-start | bytes 1572868
  2.7 34.5 %all-to-all-start = ((bf16[8,128,512]{2,1,0:T(8,128)(2,1)}), bf16[8,128,512]{2,1,0:T(8,128)(2,1)}, u32[]{:S(2)}, u32[]{:S(2)}) async-start(bf16[8,128,512]{2,1,0:T(8,128)(2,1)} %broadcast_in_dim.15), calls=%async_computation | async-start | bytes 2097152 | tf_op jit(solution)/shard_map/all_to_all | solution.py:214
  10.5 1.0 copy-start.3
  11.6 8.0 %collective-permute-start = (bf16[256,2560]{1,0:T(8,128)(2,1)S(1)}, bf16[256,2560]{1,0:T(8,128)(2,1)S(1)}, u32[]{:S(2)}, u32[]{:S(2)}) collective-permute-start(bf16[256,2560]{1,0:T(8,128)(2,1)S(1)} %pad_maximum_fusion), channel_id=1, source_target_pairs={{0,1},{1,0},{2,3},{3,2},{4,5},{5,4},{6,7},{7,6},{8,9},{9,8},{10,11... | collective-permute-start | bytes 3932168 | tf_op jit(solution)/shard_map/ppermute | solution.py:211
  19.6 1.1 copy-start.1
  89.6 14.9 %all-to-all-start.3 = ((bf16[4,4,64,512]{3,2,1,0:T(8,128)(2,1)}), bf16[4,4,64,512]{3,2,1,0:T(8,128)(2,1)S(1)}, u32[]{:S(2)}, u32[]{:S(2)}) async-start(bf16[4,4,64,512]{3,2,1,0:T(8,128)(2,1)} %get-tuple-element.35), calls=%async_computation.3 | async-start | bytes 2097152 | tf_op jit(solution)/shard_map/all_to_all | solution.py:245
  98.8 18.7 %collective-permute-start.1 = (bf16[3,256,512]{2,1,0:T(8,128)(2,1)}, bf16[3,256,512]{2,1,0:T(8,128)(2,1)S(1)}, u32[]{:S(2)}, u32[]{:S(2)}) collective-permute-start(bf16[3,256,512]{2,1,0:T(8,128)(2,1)} %get-tuple-element.28), channel_id=1, source_target_pairs={{0,1},{1,0},{2,3},{3,2},{4,5},{5,4},{6,7},{7,6},{8,9},{9,8},{10,11... | collective-permute-start | bytes 2359304 | tf_op jit(solution)/shard_map/ppermute | solution.py:211
  104.5 1.0 copy-start.4
  107.7 24.1 %all-to-all-start.4 = ((bf16[128,8,128]{2,1,0:T(8,128)(2,1)}), bf16[128,8,128]{2,1,0:T(8,128)(2,1)S(1)}, u32[]{:S(2)}, u32[]{:S(2)}) async-start(bf16[128,8,128]{2,1,0:T(8,128)(2,1)} %bitcast.27), calls=%async_computation.4 | async-start | bytes 524288 | tf_op jit(solution)/shard_map/all_to_all | solution.py:260
  117.5 0.9 copy-start.8
  131.9 0.7 copy-start.7

commit v3 on v2

--- a/solution.py
+++ b/solution.py
@@ -21,7 +21,7 @@
     return ref[:, h * HEAD : (h + 1) * HEAD]
 
 
-def call(kernel, core, ins, outs, scratch=(), vmem=60):
+def call(kernel, core, ins, outs, scratch=(), vmem=16):
     def spec(operand):
         if isinstance(operand, tuple):
             array, columns, place = operand
@@ -59,34 +59,38 @@
     return (chunk.astype(F32) + jnp.where(here, inside, 0.0)).astype(BF16)
 
 
-def local_kernel(factor, core, q, k, v, dy, far, near_state, far_state, near_out, far_out, dy_turned):
-    half = q.shape[1]
+def copies_kernel(core, w, copies):
+    for k in range(copies.shape[0]):
+        copies[k] = w[...]
+
+
+def local_kernel(factor, core, q, k, v, dy, dy_far, q_far, k_far, v_far, inside, both, out, out_far, dy_turned):
     tokens = q.shape[0]
-    q_far, k_far, v_far = (far.at[:, i * half : (i + 1) * half] for i in range(3))
-    for h in range(near_state.shape[0]):
+    for h in range(inside.shape[0]):
         at = slice(h * HEAD, (h + 1) * HEAD)
-        for qs, ks, vs, state, o in ((q, k, v, near_state, near_out), (q_far, k_far, v_far, far_state, far_out)):
+        states = []
+        for qs, ks, vs, o in ((q, k, v, out), (q_far, k_far, v_far, out_far)):
             qh, kh, vh = head(qs, h), head(ks, h), head(vs, h)
-            state[h] = dot(kh, vh, (0, 0))
+            states.append(dot(kh, vh, (0, 0)))
             o[:, at] = dot(masked(dot(qh, kh, (1, 1)), factor), vh, (1, 0))
+        inside[h] = jnp.where(core[0] == 0, states[0], states[1])
+        both[h] = (states[0] + states[1]).astype(BF16)
     dy_turned[:, :tokens] = dy[...].T
-    dy_turned[:, tokens:] = far[:, 3 * half :].T
-
-
-def d_out_kernel(core, dy, far, w, q, near_state, far_state, d, d_far, near, other, both):
-    half = q.shape[1]
+    dy_turned[:, tokens:] = dy_far[...].T
+
+
+def d_out_kernel(core, dy, dy_far, w, q, q_far, states, d, d_far, inside, both):
     d[...] = dot(dy[...], w[...], (1, 0)).astype(BF16)
-    d_far[...] = dot(far[:, 3 * half :], w[...], (1, 0)).astype(BF16)
-    chips, lines, _ = both.shape
+    d_far[...] = dot(dy_far[...], w[...], (1, 0)).astype(BF16)
+    _, lines, _ = both.shape
     lines = lines // 2
     per_head = HEAD // lines
-    for h in range(near.shape[0]):
+    for h in range(inside.shape[0]):
         g = dot(head(q, h), head(d, h), (0, 0))
-        g_far = dot(head(far, h), head(d_far, h), (0, 0))
-        near[h] = g
-        other[h] = g_far
-        for side, total in ((0, near_state[h] + far_state[h]), (1, g + g_far)):
-            total = total.astype(BF16).reshape(per_head, lines, HEAD)
+        g_far = dot(head(q_far, h), head(d_far, h), (0, 0))
+        inside[h] = jnp.where(core[0] == 0, g_far, g)
+        for side, total in ((0, states[h]), (1, (g + g_far).astype(BF16))):
+            total = total.reshape(per_head, lines, HEAD)
             both[h * per_head : (h + 1) * per_head, side * lines : (side + 1) * lines, :] = total
 
 
@@ -107,42 +111,34 @@
     return sums[h * per_head : (h + 1) * per_head, side * lines : (side + 1) * lines, :].reshape(HEAD, HEAD)
 
 
-def output_kernel(factor, core, q, far, sums, s_near, s_far, local, local_far, dy_turned, weight, out, held):
+def output_kernel(factor, core, q, q_far, sums, s_in, local, local_far, dy_turned, weight, out, held):
     tokens = q.shape[0]
-    for h in range(s_near.shape[0]):
+    for h in range(s_in.shape[0]):
         at = slice(h * HEAD, (h + 1) * HEAD)
         prior = chunk_sum(sums, h, 0)
-        for qs, inside, here, part, rows in (
-            (q, s_far, core[0] == 1, local, slice(0, tokens)),
-            (far, s_near, core[0] == 0, local_far, slice(tokens, 2 * tokens)),
-        ):
-            before = entering(prior, inside[h], here)
-            out[rows, at] = (part[:, at] + factor * dot(head(qs, h), before, (1, 0))).astype(BF16)
+        for side, (qs, part) in enumerate(((q, local), (q_far, local_far))):
+            before = entering(prior, s_in[h], core[0] == 1 - side)
+            whole = part[:, at] + factor * dot(head(qs, h), before, (1, 0))
+            out[side * tokens : (side + 1) * tokens, at] = whole.astype(BF16)
     whole = dot(dy_turned[...], out[...], (1, 0))
-    for b in range(s_near.shape[0]):
+    for b in range(s_in.shape[0]):
         held[b] = whole[:, b * HEAD : (b + 1) * HEAD]
     places, lines, count, _ = weight.shape
     for x in range(places):
         for t in range(lines):
-            for b in range(s_near.shape[0]):
+            for b in range(s_in.shape[0]):
                 at = slice(b * HEAD, (b + 1) * HEAD)
                 weight[x, t, :, at] = held[b, pl.ds(x * lines + t, count, stride=places * lines), :].astype(BF16)
 
 
-def grads_kernel(factor, core, q, k, v, far, d, d_far, sums, s_near, s_far, g_near, g_far, near, other):
-    first = core[0] == 0
-    half = q.shape[1]
-    q_far, k_far, v_far = (far.at[:, i * half : (i + 1) * half] for i in range(3))
-    for h in range(s_near.shape[0]):
+def grads_kernel(factor, core, q, k, v, q_far, k_far, v_far, d, d_far, sums, s_in, g_in, near, other):
+    for h in range(s_in.shape[0]):
         at = slice(h * HEAD, (h + 1) * HEAD)
         prior, later = chunk_sum(sums, h, 0), chunk_sum(sums, h, 1)
-        for qs, ks, vs, ds, s_in, s_here, g_in, g_here, o in (
-            (q, k, v, d, s_far, core[0] == 1, g_far, first, near),
-            (q_far, k_far, v_far, d_far, s_near, first, g_near, core[0] == 1, other),
-        ):
+        for side, (qs, ks, vs, ds, o) in enumerate(((q, k, v, d, near), (q_far, k_far, v_far, d_far, other))):
             qh, kh, vh, dh = head(qs, h), head(ks, h), head(vs, h), head(ds, h)
-            before = entering(prior, s_in[h], s_here)
-            after = entering(later, g_in[h], g_here)
+            before = entering(prior, s_in[h], core[0] == 1 - side)
+            after = entering(later, g_in[h], core[0] == side)
             scores = masked(dot(qh, kh, (1, 1)), factor)
             score_grad = masked(dot(dh, vh, (1, 1)), factor)
             o[0, :, at] = (dot(score_grad, kh, (1, 0)) + factor * dot(dh, before, (1, 1))).astype(BF16)
@@ -210,26 +206,31 @@
     def swap(a):
         return lax.ppermute(a, "c", ((0, 1), (1, 0)))
 
-    copies = jnp.broadcast_to(halves(out_weight, c)[None], (sizes["y"], width // sizes["y"], half))
+    (copies,) = call(
+        copies_kernel, core, [(out_weight, half, None)], [shape((sizes["y"], width // sizes["y"], half), BF16)], vmem=60
+    )
     w = lax.all_to_all(copies, "y", 0, 0).reshape(width, half)
-    far = swap(jnp.concatenate([halves(q, 1 - c), halves(k, 1 - c), halves(v, 1 - c), dy], 1))
+    far = swap(jnp.concatenate([dy, halves(q, 1 - c), halves(k, 1 - c), halves(v, 1 - c)], 1))
     own = [(a, half, None) for a in (q, k, v)]
-
-    state = shape((heads, HEAD, HEAD), F32)
+    dy_far = (far, width, 0)
+    others = [(far, half, width // half + i) for i in range(3)]
+
+    inside = shape((heads, HEAD, HEAD), F32)
     tokens = shape((stretch, half), BF16)
     part = shape((stretch, half), F32)
-    s_near, s_far, local, local_far, dy_turned = call(
+    s_in, s_both, local, local_far, dy_turned = call(
         functools.partial(local_kernel, factor),
         core,
-        own + [dy, far],
-        [state, state, part, part, shape((width, 2 * stretch), BF16)],
+        own + [dy, dy_far] + others,
+        [inside, shape(inside.shape, BF16), part, part, shape((width, 2 * stretch), BF16)],
+        vmem=24,
     )
     slices = shape((chips, 2 * heads * HEAD // chips, HEAD), BF16)
-    d, d_far, g_near, g_far, both = call(
-        d_out_kernel, core, [dy, far, w, own[0], s_near, s_far], [tokens, tokens, state, state, slices]
+    d, d_far, g_in, both = call(
+        d_out_kernel, core, [dy, dy_far, w, own[0], others[0], s_both], [tokens, tokens, inside, slices], vmem=16
     )
     both = lax.all_to_all(both, ("z", "x"), 0, 0)
-    (sums,) = call(prefix_kernel, core, [both], [slices])
+    (sums,) = call(prefix_kernel, core, [both], [slices], vmem=3)
     sums = lax.all_to_all(sums, ("z", "x"), 0, 0)
 
     rows = width // sizes["y"] // (chips * 2)
@@ -238,9 +239,10 @@
     partial, _ = call(
         functools.partial(output_kernel, factor),
         core,
-        [own[0], far, sums, s_near, s_far, local, local_far, dy_turned],
+        [own[0], others[0], sums, s_in, local, local_far, dy_turned],
         [shape((sizes["x"], 2 * rows, places, half), BF16), shape((2 * stretch, half), BF16)],
         [pltpu.VMEM((blocks, width, HEAD), F32)],
+        vmem=24,
     )
     parts = lax.all_to_all(partial, "x", 0, 0)
 
@@ -248,15 +250,16 @@
     near, other = call(
         functools.partial(grads_kernel, factor),
         core,
-        own + [far, d, d_far, sums, s_near, s_far, g_near, g_far],
+        own + others + [d, d_far, sums, s_in, g_in],
         [grads, grads],
+        vmem=60,
     )
     back = swap(other)
     whole = shape((stretch, width), BF16)
-    q_grad, k_grad, v_grad = call(join_kernel, core, [near, back], [whole] * 3)
+    q_grad, k_grad, v_grad = call(join_kernel, core, [near, back], [whole] * 3, vmem=10)
 
     lines = shape((places * 2 * rows * blocks, HEAD), BF16)
-    (summed,) = call(gather_rows_kernel, core, [parts], [lines], [pltpu.VMEM(lines.shape, F32)])
+    (summed,) = call(gather_rows_kernel, core, [parts], [lines], [pltpu.VMEM(lines.shape, F32)], vmem=8)
     summed = lax.all_to_all(summed.reshape(places * 2, rows * blocks, HEAD), ("y", "z", "c"), 0, 0)
     (weight_grad,) = call(
         functools.partial(sum_kernel, grad_factor),
@@ -264,6 +267,7 @@
         [summed],
         [shape((rows, width), F32)],
         [pltpu.VMEM((rows * blocks, HEAD), F32)],
+        vmem=3,
     )
     return q_grad[None], k_grad[None], v_grad[None], weight_grad
 

time: 135 us -> 124 us (0.919)
  Pallas kernels: 27.1 us -> 15.7 us
  waiting for transfers between devices: 25.3 us -> 29.2 us
  local copies, waits for them, and re-layouts: 6.67 us -> 4.33 us
    pallas_call x8 -> x9, Pallas kernels: 27.1 us -> 15.7 us  [call(): pl.pallas_call(kernel, grid_spec=pltpu.PrefetchScalarGridSpec(num_scalar_...]
    all_to_all x1, waiting for transfers between devices: 10.8 us -> 13 us  [per_device(): lax.all_to_all(summed.reshape(places * 2, rows * blocks, HEAD), ('y', 'z'...]
    all_to_all x1, waiting for transfers between devices: 11.9 us -> 13.5 us  [per_device(): w = lax.all_to_all(copies, 'y', 0, 0).reshape(width, half)]
    unnamed x18 -> x40, local copies, waits for them, and re-layouts: 5.52 us -> 4.26 us
  transfers between devices with their start and end apart: 5 -> 5, of which waited for: 3 -> 3; matrix products, arithmetic and copies ran while one was open for 0% -> 0% of each run, Pallas kernels for 11% -> 8%
where the time goes in v3:
time: 124 us; the launch traced here: 123 us
  blocking collectives  41.1 us (33%)
  starting transfers between devices  31.9 us (26%)
  waiting for transfers between devices  29.2 us (24%)
  Pallas kernels  15.7 us (13%)
  local copies, waits for them, and re-layouts  4.33 us (3%)
    all_to_all x1, blocking collectives, per_device(): both = lax.all_to_all(both, ('z', 'x'), 0, 0)  26.3 us
    pallas_call x9, Pallas kernels, call(): pl.pallas_call(kernel, grid_spec=pltpu.PrefetchScalarGridSpec(num_scalar_...  15.7 us
    all_to_all x1, blocking collectives, per_device(): sums = lax.all_to_all(sums, ('z', 'x'), 0, 0)  14.8 us
    all_to_all x1, waiting for transfers between devices, per_device(): w = lax.all_to_all(copies, 'y', 0, 0).reshape(width, half)  13.5 us
    all_to_all x1, waiting for transfers between devices, per_device(): lax.all_to_all(summed.reshape(places * 2, rows * blocks, HEAD), ('y', 'z'...  13 us
    ppermute x2, starting transfers between devices, swap(): return lax.ppermute(a, 'c', ((0, 1), (1, 0)))  10.5 us
    all_to_all x1, starting transfers between devices, per_device(): lax.all_to_all(summed.reshape(places * 2, rows * blocks, HEAD), ('y', 'z'...  10 us
    all_to_all x1, starting transfers between devices, per_device(): w = lax.all_to_all(copies, 'y', 0, 0).reshape(width, half)  7.78 us
  transfers between devices with their start and end apart: 5, of which 3 were waited for; matrix products, arithmetic and copies ran while one was open for 0% of the time, Pallas kernels for 8%

profile of v3, /device:TPU:1, one launch (start us, length us, event | category | flops | bytes accessed | tf_op | source)
XLA Modules:
  0.0 123.2 jit_solution(10842238340314681756)
XLA Ops:
  0.6 1.9 %shard_map.84 = bf16[8,128,512]{2,1,0:T(8,128)(2,1)} custom-call(s32[1]{0:T(128)} %bitcast.core, bf16[128,1024]{1,0:T(8,128)(2,1)} %w.1), custom_call_target="tpu_custom_call" | custom-call | tf_op jit(solution)/shard_map/pallas_call | solution.py:34
  2.6 0.0 copy-start.1
  2.6 0.0 copy-start.3
  2.6 0.0 copy-start.5
  2.6 7.8 %all-to-all-start = ((bf16[8,128,512]{2,1,0:T(8,128)(2,1)}), bf16[8,128,512]{2,1,0:T(8,128)(2,1)S(1)}, u32[]{:S(2)}, u32[]{:S(2)}) async-start(bf16[8,128,512]{2,1,0:T(8,128)(2,1)} %shard_map.84), calls=%async_computation | async-start | bytes 2097152 | tf_op jit(solution)/shard_map/all_to_all | solution.py:212
  10.4 0.0 copy-start.2
  10.4 0.0 copy-done.1
  10.4 0.0 copy-done.3
  10.4 0.0 copy-done.5
  10.5 0.9 copy-done.2
  11.4 0.0 copy-start.4
  11.4 0.0 copy-start.6
  11.4 0.1 pad_maximum_fusion
  11.5 4.8 %collective-permute-start = (bf16[256,2560]{1,0:T(8,128)(2,1)S(1)}, bf16[256,2560]{1,0:T(8,128)(2,1)S(1)}, u32[]{:S(2)}, u32[]{:S(2)}) collective-permute-start(bf16[256,2560]{1,0:T(8,128)(2,1)S(1)} %pad_maximum_fusion), channel_id=1, source_target_pairs={{0,1},{1,0},{2,3},{3,2},{4,5},{5,4},{6,7},{7,6},{8,9},{9,8},{10,11... | collective-permute-start | bytes 3932168 | tf_op jit(solution)/shard_map/ppermute | solution.py:207
  16.3 2.6 %collective-permute-done.dy_far.q_far.k_far.v_far = bf16[256,2560]{1,0:T(8,128)(2,1)S(1)} collective-permute-done((bf16[256,2560]{1,0:T(8,128)(2,1)S(1)}, bf16[256,2560]{1,0:T(8,128)(2,1)S(1)}, u32[]{:S(2)}, u32[]{:S(2)}) %collective-permute-start) | collective-permute-done | bytes 1310752 | tf_op jit(solution)/shard_map/ppermute | solution.py:207
  19.0 0.0 copy-start
  19.0 0.0 copy-done.4
  19.0 0.0 copy-done.6
  19.0 1.7 %shard_map.85 = (f32[4,128,128]{2,1,0:T(8,128)S(1)}, bf16[4,128,128]{2,1,0:T(8,128)(2,1)S(1)}, f32[256,512]{1,0:T(8,128)S(1)}, f32[256,512]{1,0:T(8,128)S(1)}, bf16[1024,512]{1,0:T(8,128)(2,1)S(1)}) custom-call(s32[1]{0:T(128)} %bitcast.core, bf16[256,1024]{1,0:T(8,128)(2,1)S(1)} %bitcast.17, bf16[256,1024]{1,0:T(8,128)(2,1)S(1)} %bitcast.25, ...), custom_call_target="tpu_custom_call" | custom-call | tf_op jit(solution)/shard_map/pallas_call | solution.py:34
  20.7 0.0 copy-start.8
  20.7 1.0 copy-done.8
  21.7 0.0 copy-start.10
  21.7 0.7 copy-done.10
  22.4 0.0 copy-start.13
  22.4 0.8 copy-done.13
  23.2 0.0 copy-start.15
  23.2 0.8 copy-done.15
  24.0 13.5 %all-to-all-done = bf16[8,128,512]{2,1,0:T(8,128)(2,1)S(1)} async-done(((bf16[8,128,512]{2,1,0:T(8,128)(2,1)}), bf16[8,128,512]{2,1,0:T(8,128)(2,1)S(1)}, u32[]{:S(2)}, u32[]{:S(2)}) %all-to-all-start) | async-done | bytes 1048608 | tf_op jit(solution)/shard_map/all_to_all | solution.py:212
  37.5 0.0 copy-start.14
  37.6 0.0 copy-start.16
  37.6 1.0 shard_map.86
  38.6 0.0 copy-start.17
  38.6 0.0 copy-start.18
  38.6 0.0 copy-start.19
  38.6 0.0 copy-start.9
  38.6 0.0 copy-start.11
  38.6 26.3 %all_to_all.25.terms = bf16[32,32,128]{2,1,0:T(8,128)(2,1)S(1)} all-to-all(bf16[32,32,128]{2,1,0:T(8,128)(2,1)S(1)} %get-tuple-element.22), channel_id=1, replica_groups=mesh['y'=8,'z'=8,'x'=4,'c'=2] {'z','x'}, dimensions={0} | all-to-all | bytes 524288 | tf_op jit(solution)/shard_map/all_to_all | solution.py:232
  65.0 14.8 %all_to_all.26.sums = bf16[32,32,128]{2,1,0:T(8,128)(2,1)S(1)} all-to-all(bf16[32,32,128]{2,1,0:T(8,128)(2,1)S(1)} %shard_map.87), channel_id=1, replica_groups=mesh['y'=8,'z'=8,'x'=4,'c'=2] {'z','x'}, dimensions={0} | all-to-all | bytes 524288 | tf_op jit(solution)/shard_map/all_to_all | solution.py:234
  79.8 0.0 copy-done.17
  79.8 0.0 copy-start.7
  79.8 0.0 copy-done.18
  79.8 0.0 copy-done.19
  79.8 0.0 copy-done
  79.8 0.0 copy-done.14
  79.8 0.0 copy-done.16
  79.8 0.0 copy-done.9
  79.8 0.0 copy-done.11
  79.8 2.6 %shard_map.90 = (bf16[4,4,64,512]{3,2,1,0:T(8,128)(2,1)}, bf16[512,512]{1,0:T(8,128)(2,1)}) custom-call(s32[1]{0:T(128)} %bitcast.core, bf16[256,1024]{1,0:T(8,128)(2,1)S(1)} %bitcast.19, bf16[256,2560]{1,0:T(8,128)(2,1)S(1)} %collective-permute-done.dy_far.q_far.k_far.v_far, bf16[32,32,128]{2,1,0:T(8,128)(2,1)S(1)} %all_to_all.26.sums, ...), custom_call_target="tpu_custom_call" | custom-call | tf_op jit(solution)/shard_map/pallas_call | solution.py:34
  82.4 0.0 copy-done.7
  82.4 3.5 %all-to-all-start.3 = ((bf16[4,4,64,512]{3,2,1,0:T(8,128)(2,1)}), bf16[4,4,64,512]{3,2,1,0:T(8,128)(2,1)S(1)}, u32[]{:S(2)}, u32[]{:S(2)}) async-start(bf16[4,4,64,512]{3,2,1,0:T(8,128)(2,1)} %get-tuple-element.33), calls=%async_computation.3 | async-start | bytes 2097152 | tf_op jit(solution)/shard_map/all_to_all | solution.py:247
  86.0 5.4 %shard_map.88 = (bf16[3,256,512]{2,1,0:T(8,128)(2,1)}, bf16[3,256,512]{2,1,0:T(8,128)(2,1)}) custom-call(s32[1]{0:T(128)} %bitcast.core, bf16[256,1024]{1,0:T(8,128)(2,1)} %bitcast.16, bf16[256,1024]{1,0:T(8,128)(2,1)} %bitcast.24, bf16[256,1024]{1,0:T(8,128)(2,1)} %bitcast.26, bf16[256,2560]{1,0:T(8,128)(2,1)} %copy-done, bf16[256,2560]{1,0:T(8,128)(2,1)} %copy-done, ...), custom_call_target="tpu_custom_call" | custom-call | tf_op jit(solution)/shard_map/pallas_call | solution.py:34
  91.4 0.0 copy-start.12
  91.4 5.7 %collective-permute-start.1 = (bf16[3,256,512]{2,1,0:T(8,128)(2,1)}, bf16[3,256,512]{2,1,0:T(8,128)(2,1)S(1)}, u32[]{:S(2)}, u32[]{:S(2)}) collective-permute-start(bf16[3,256,512]{2,1,0:T(8,128)(2,1)} %get-tuple-element.26), channel_id=1, source_target_pairs={{0,1},{1,0},{2,3},{3,2},{4,5},{5,4},{6,7},{7,6},{8,9},{9,8},{10,11... | collective-permute-start | bytes 2359304 | tf_op jit(solution)/shard_map/ppermute | solution.py:207
  97.1 0.0 all-to-all-done.3.parts
  97.1 1.0 shard_map.91
  98.1 10.0 %all-to-all-start.4 = ((bf16[128,8,128]{2,1,0:T(8,128)(2,1)}), bf16[128,8,128]{2,1,0:T(8,128)(2,1)S(1)}, u32[]{:S(2)}, u32[]{:S(2)}) async-start(bf16[128,8,128]{2,1,0:T(8,128)(2,1)} %bitcast.12), calls=%async_computation.4 | async-start | bytes 524288 | tf_op jit(solution)/shard_map/all_to_all | solution.py:263
  108.1 0.0 collective-permute-done.1.far
  108.2 0.0 copy-done.12
  108.2 1.3 %shard_map.89 = (bf16[256,1024]{1,0:T(8,128)(2,1)}, bf16[256,1024]{1,0:T(8,128)(2,1)}, bf16[256,1024]{1,0:T(8,128)(2,1)}) custom-call(s32[1]{0:T(128)} %bitcast.core, bf16[3,256,512]{2,1,0:T(8,128)(2,1)S(1)} %copy-done.12, bf16[3,256,512]{2,1,0:T(8,128)(2,1)S(1)} %collective-permute-done.1.far), custom_call_target="tpu_custom_call" | custom-call | tf_op jit(solution)/shard_map/pallas_call | solution.py:34
  109.4 13.0 %all-to-all-done.4.parts = bf16[128,8,128]{2,1,0:T(8,128)(2,1)S(1)} async-done(((bf16[128,8,128]{2,1,0:T(8,128)(2,1)}), bf16[128,8,128]{2,1,0:T(8,128)(2,1)S(1)}, u32[]{:S(2)}, u32[]{:S(2)}) %all-to-all-start.4) | async-done | bytes 262176 | tf_op jit(solution)/shard_map/all_to_all | solution.py:263
  122.5 0.7 shard_map.92
  (3 shorter events, 0.1 us)
Async XLA Ops:
  2.6 7.8 %copy-start.1 = (bf16[1,256,1024]{2,1,0:T(8,128)(2,1)S(1)}, bf16[1,256,1024]{2,1,0:T(8,128)(2,1)}, u32[]{:S(2)}) copy-start(bf16[1,256,1024]{2,1,0:T(8,128)(2,1)} %param.5) | copy-start | bytes 1572868
  2.6 7.8 %copy-start.3 = (bf16[1,256,1024]{2,1,0:T(8,128)(2,1)S(1)}, bf16[1,256,1024]{2,1,0:T(8,128)(2,1)}, u32[]{:S(2)}) copy-start(bf16[1,256,1024]{2,1,0:T(8,128)(2,1)} %param.6) | copy-start | bytes 1572868
  2.6 7.8 %copy-start.5 = (bf16[1,256,1024]{2,1,0:T(8,128)(2,1)S(1)}, bf16[1,256,1024]{2,1,0:T(8,128)(2,1)}, u32[]{:S(2)}) copy-start(bf16[1,256,1024]{2,1,0:T(8,128)(2,1)} %param.7) | copy-start | bytes 1572868
  2.6 35.0 %all-to-all-start = ((bf16[8,128,512]{2,1,0:T(8,128)(2,1)}), bf16[8,128,512]{2,1,0:T(8,128)(2,1)S(1)}, u32[]{:S(2)}, u32[]{:S(2)}) async-start(bf16[8,128,512]{2,1,0:T(8,128)(2,1)} %shard_map.84), calls=%async_computation | async-start | bytes 2097152 | tf_op jit(solution)/shard_map/all_to_all | solution.py:212
  10.4 1.0 copy-start.2
  11.4 7.6 %copy-start.4 = (bf16[1,256,1024]{2,1,0:T(8,128)(2,1)S(1)}, bf16[1,256,1024]{2,1,0:T(8,128)(2,1)}, u32[]{:S(2)}) copy-start(bf16[1,256,1024]{2,1,0:T(8,128)(2,1)} %param.6) | copy-start | bytes 1572868
  11.4 7.6 %copy-start.6 = (bf16[1,256,1024]{2,1,0:T(8,128)(2,1)S(1)}, bf16[1,256,1024]{2,1,0:T(8,128)(2,1)}, u32[]{:S(2)}) copy-start(bf16[1,256,1024]{2,1,0:T(8,128)(2,1)} %param.7) | copy-start | bytes 1572868
  11.5 7.5 %collective-permute-start = (bf16[256,2560]{1,0:T(8,128)(2,1)S(1)}, bf16[256,2560]{1,0:T(8,128)(2,1)S(1)}, u32[]{:S(2)}, u32[]{:S(2)}) collective-permute-start(bf16[256,2560]{1,0:T(8,128)(2,1)S(1)} %pad_maximum_fusion), channel_id=1, source_target_pairs={{0,1},{1,0},{2,3},{3,2},{4,5},{5,4},{6,7},{7,6},{8,9},{9,8},{10,11... | collective-permute-start | bytes 3932168 | tf_op jit(solution)/shard_map/ppermute | solution.py:207
  19.0 60.8 %copy-start = (bf16[256,2560]{1,0:T(8,128)(2,1)}, bf16[256,2560]{1,0:T(8,128)(2,1)S(1)}, u32[]{:S(2)}) copy-start(bf16[256,2560]{1,0:T(8,128)(2,1)S(1)} %collective-permute-done.dy_far.q_far.k_far.v_far) | copy-start | bytes 3932164
  20.7 1.0 copy-start.8
  21.7 0.7 copy-start.10
  22.4 0.8 copy-start.13
  23.2 0.8 copy-start.15
  37.5 42.3 %copy-start.14 = (f32[256,512]{1,0:T(8,128)S(1)}, f32[256,512]{1,0:T(8,128)}, u32[]{:S(2)}) copy-start(f32[256,512]{1,0:T(8,128)} %copy-done.13) | copy-start | bytes 1572868
  37.6 42.3 %copy-start.16 = (f32[256,512]{1,0:T(8,128)S(1)}, f32[256,512]{1,0:T(8,128)}, u32[]{:S(2)}) copy-start(f32[256,512]{1,0:T(8,128)} %copy-done.15) | copy-start | bytes 1572868
  38.6 41.2 %copy-start.17 = (bf16[256,512]{1,0:T(8,128)(2,1)}, bf16[256,512]{1,0:T(8,128)(2,1)S(1)}, u32[]{:S(2)}) copy-start(bf16[256,512]{1,0:T(8,128)(2,1)S(1)} %get-tuple-element.20.d) | copy-start | bytes 786436
  38.6 41.2 %copy-start.18 = (bf16[256,512]{1,0:T(8,128)(2,1)}, bf16[256,512]{1,0:T(8,128)(2,1)S(1)}, u32[]{:S(2)}) copy-start(bf16[256,512]{1,0:T(8,128)(2,1)S(1)} %get-tuple-element.21.d_far) | copy-start | bytes 786436
  38.6 41.2 %copy-start.19 = (f32[4,128,128]{2,1,0:T(8,128)}, f32[4,128,128]{2,1,0:T(8,128)S(1)}, u32[]{:S(2)}) copy-start(f32[4,128,128]{2,1,0:T(8,128)S(1)} %get-tuple-element.24.g_in) | copy-start | bytes 786436
  38.6 41.2 %copy-start.9 = (bf16[1024,512]{1,0:T(8,128)(2,1)S(1)}, bf16[1024,512]{1,0:T(8,128)(2,1)}, u32[]{:S(2)}) copy-start(bf16[1024,512]{1,0:T(8,128)(2,1)} %copy-done.8) | copy-start | bytes 3145732
  38.6 41.2 %copy-start.11 = (f32[4,128,128]{2,1,0:T(8,128)S(1)}, f32[4,128,128]{2,1,0:T(8,128)}, u32[]{:S(2)}) copy-start(f32[4,128,128]{2,1,0:T(8,128)} %copy-done.10) | copy-start | bytes 786436
  79.8 2.6 %copy-start.7 = (bf16[32,32,128]{2,1,0:T(8,128)(2,1)}, bf16[32,32,128]{2,1,0:T(8,128)(2,1)S(1)}, u32[]{:S(2)}) copy-start(bf16[32,32,128]{2,1,0:T(8,128)(2,1)S(1)} %all_to_all.26.sums) | copy-start | bytes 786436
  82.4 14.7 %all-to-all-start.3 = ((bf16[4,4,64,512]{3,2,1,0:T(8,128)(2,1)}), bf16[4,4,64,512]{3,2,1,0:T(8,128)(2,1)S(1)}, u32[]{:S(2)}, u32[]{:S(2)}) async-start(bf16[4,4,64,512]{3,2,1,0:T(8,128)(2,1)} %get-tuple-element.33), calls=%async_computation.3 | async-start | bytes 2097152 | tf_op jit(solution)/shard_map/all_to_all | solution.py:247
  91.4 16.8 %copy-start.12 = (bf16[3,256,512]{2,1,0:T(8,128)(2,1)S(1)}, bf16[3,256,512]{2,1,0:T(8,128)(2,1)}, u32[]{:S(2)}) copy-start(bf16[3,256,512]{2,1,0:T(8,128)(2,1)} %get-tuple-element.25.near) | copy-start | bytes 2359300
  91.4 16.8 %collective-permute-start.1 = (bf16[3,256,512]{2,1,0:T(8,128)(2,1)}, bf16[3,256,512]{2,1,0:T(8,128)(2,1)S(1)}, u32[]{:S(2)}, u32[]{:S(2)}) collective-permute-start(bf16[3,256,512]{2,1,0:T(8,128)(2,1)} %get-tuple-element.26), channel_id=1, source_target_pairs={{0,1},{1,0},{2,3},{3,2},{4,5},{5,4},{6,7},{7,6},{8,9},{9,8},{10,11... | collective-permute-start | bytes 2359304 | tf_op jit(solution)/shard_map/ppermute | solution.py:207
  98.1 24.4 %all-to-all-start.4 = ((bf16[128,8,128]{2,1,0:T(8,128)(2,1)}), bf16[128,8,128]{2,1,0:T(8,128)(2,1)S(1)}, u32[]{:S(2)}, u32[]{:S(2)}) async-start(bf16[128,8,128]{2,1,0:T(8,128)(2,1)} %bitcast.12), calls=%async_computation.4 | async-start | bytes 524288 | tf_op jit(solution)/shard_map/all_to_all | solution.py:263
